TPU v7x, 32 devices: a whole 2x2x4 slice. The times are simulated.
32 devices in a mesh: groups: 2 (over y), pb: 16 (over z, x, core).
Axes of the slice: x: 2, y: 2, z: 4, core: 2. Of those that a mesh axis runs over, the one named last changes fastest.
Arguments:
- fields: float32 [32, 16, 512], P(('groups', 'pb')), parts along dimension 0, may hold values from -6 to 6
- field_shift: float32 [16, 512], replicated, may hold values from -1 to 1
- cholesky: bfloat16 [512, 1024, 1024], P(None, 'pb'), may hold values from -0.015625 to 0.015625
- onebody: float32 [16, 64], replicated, may hold values from -0.5 to 0.5
- walkers: bfloat16 [32, 1024, 256], P(('groups', 'pb')), parts along dimension 0, may hold values from -6 to 6
Outputs:
- propagated: bfloat16 [32, 1024, 256], P(('groups', 'pb')), parts along dimension 0
There are 2 independent parts, one for each index of `groups`. A program takes and returns all parts, laid end to end along the dimension named above; an argument that names none is the same for every part. Nothing has to cross between parts.
All inputs are finite; a program needn't handle non-finite values.
Results may differ from a plain program's by a relative error of at most 0.0089.
Values may be sent and summed in bfloat16 or wider, within the bound.
No kernel may reach another device: no remote copies, remote signals or barrier semaphores. Data moves between devices by JAX's collectives and lax.ppermute only.
A program may use at most 192 MiB of HBM per device.

v0:
```python
import jax
import jax.numpy as jnp
import numpy as np
from jax import lax
from jax.sharding import PartitionSpec as P

TERMS = 6


def per_device(fields, field_shift, cholesky, onebody, walkers):
    devices = lax.axis_size("pb")
    local_walkers = fields.shape[0]
    kpoints = field_shift.shape[0]
    orbitals = onebody.shape[1]
    vectors = field_shift.shape[1]
    rows_here = cholesky.shape[1]
    per_transfer = orbitals // rows_here
    slab = cholesky.reshape(vectors, rows_here * kpoints * orbitals)
    shifted = (fields + field_shift[None]).astype(jnp.bfloat16)
    outgoing = jnp.repeat(shifted, per_transfer, axis=1)
    arrived = lax.all_to_all(outgoing, "pb", split_axis=1, concat_axis=0, tiled=True)
    partial_blocks = jnp.dot(arrived[:, 0, :], slab, preferred_element_type=jnp.float32).astype(
        jnp.bfloat16
    )
    outgoing_blocks = partial_blocks.reshape(devices, local_walkers, rows_here * kpoints * orbitals)
    relayed = lax.all_to_all(outgoing_blocks, "pb", split_axis=0, concat_axis=0, tiled=True)
    relayed = relayed.reshape(kpoints, per_transfer, local_walkers, rows_here, kpoints, orbitals)
    potential = relayed.transpose(2, 4, 1, 3, 0, 5).reshape(
        local_walkers, kpoints, orbitals, kpoints, orbitals
    )
    source_table = (np.arange(kpoints)[:, None] - np.arange(kpoints)[None, :]) % kpoints
    source_index = jnp.asarray(source_table.reshape(1, kpoints, 1, kpoints, 1), dtype=jnp.int32)
    permuted = jnp.take_along_axis(potential, source_index, axis=3)
    permuted = permuted.reshape(local_walkers, kpoints * orbitals, kpoints * orbitals)
    diagonal_term = onebody.reshape(kpoints * orbitals)[None, :, None]
    term = walkers
    total = term.astype(jnp.float32)
    for order in range(1, TERMS):
        product = jnp.einsum("wij,wjc->wic", permuted, term, preferred_element_type=jnp.float32)
        product = product + diagonal_term * term.astype(jnp.float32)
        term = (product * (-1.0 / order)).astype(jnp.bfloat16)
        total = total + term.astype(jnp.float32)
    return total.astype(jnp.bfloat16)


def solution(mesh):
    return jax.shard_map(
        per_device,
        mesh=mesh,
        in_specs=(
            P(("groups", "pb"), None, None),
            P(),
            P(None, "pb", None),
            P(),
            P(("groups", "pb"), None, None),
        ),
        out_specs=P(("groups", "pb"), None, None),
        check_vma=False,
    )
```

profile of v0, /device:TPU:15, one launch (start us, length us, event | category | flops | bytes accessed | tf_op | source)
XLA Modules:
  0.0 204.7 jit_solution(11339887598965163888)
XLA Ops:
  0.0 0.8 fusion.27
  0.8 0.5 broadcast.63
  1.3 0.7 reduce.1
  2.0 0.6 reshape.144
  2.6 6.6 %all-to-all-start = ((bf16[16,2,256]{2,1,0:T(2,128)(2,1)}), bf16[16,2,256]{2,1,0:T(2,128)(2,1)S(1)}, u32[]{:S(2)}, u32[]{:S(2)}) async-start(bf16[16,2,256]{2,1,0:T(2,128)(2,1)} %reshape.144), calls=%async_computation | async-start | bytes 32768 | tf_op jit(solution)/shard_map/all_to_all | solution.py:21
  9.2 58.5 %copy.17 = bf16[64,8,64,1024]{3,1,2,0:T(8,128)(2,1)} copy(bf16[64,8,64,1024]{3,2,1,0:T(8,128)(2,1)} %bitcast.17) | data formatting | bytes 134217728
  67.7 0.0 all-to-all-done
  67.7 22.8 %fusion = bf16[16,1,65536]{2,0,1:T(8,128)(2,1)S(1)} fusion(bf16[512,65536]{1,0:T(8,128)(2,1)} %bitcast.18, bf16[1,16,512]{2,0,1:T(2,128)(2,1)S(1)} %bitcast.91), kind=kOutput, calls=%fused_computation.2 | convolution fusion | flops 1074790400 | bytes 69222400 | tf_op jit(solution)/shard_map/dot_general | solution.py:22
  90.5 2.8 %reduce.2 = bf16[16,65536]{1,0:T(8,128)(2,1)} reduce(bf16[16,1,65536]{2,0,1:T(8,128)(2,1)S(1)} %fusion, bf16[]{:T(256)} %broadcast.63), dimensions={1}, to_apply=%copy.13.reduce_sub_computation | reduce | bytes 4194306 | tf_op jit(solution)/shard_map/reshape | solution.py:25
  93.3 4.0 %reshape.146 = bf16[16,2,32768]{2,1,0:T(2,128)(2,1)} reshape(bf16[16,65536]{1,0:T(8,128)(2,1)} %reduce.2) | data formatting | bytes 4194304
  97.3 0.0 copy-start.1
  97.3 6.1 %all-to-all-start.1 = ((bf16[16,2,32768]{2,1,0:T(2,128)(2,1)}), bf16[16,2,32768]{2,1,0:T(2,128)(2,1)S(1)}, u32[]{:S(2)}, u32[]{:S(2)}) async-start(bf16[16,2,32768]{2,1,0:T(2,128)(2,1)} %reshape.146), calls=%async_computation.1 | async-start | bytes 4194304 | tf_op jit(solution)/shard_map/all_to_all | solution.py:26
  103.5 0.0 copy-done.1
  103.5 0.1 mul.64
  103.6 47.3 %all-to-all-done.1 = bf16[16,2,32768]{2,1,0:T(2,128)(2,1)S(1)} async-done(((bf16[16,2,32768]{2,1,0:T(2,128)(2,1)}), bf16[16,2,32768]{2,1,0:T(2,128)(2,1)S(1)}, u32[]{:S(2)}, u32[]{:S(2)}) %all-to-all-start.1) | async-done | bytes 2097184 | tf_op jit(solution)/shard_map/all_to_all | solution.py:26
  150.9 6.8 %reshape.147 = bf16[16,1,65536]{2,1,0:T(2,128)(2,1)} reshape(bf16[16,2,32768]{2,1,0:T(2,128)(2,1)S(1)} %all-to-all-done.1) | data formatting | bytes 4194304
  157.7 12.4 %reduce = bf16[16,65536]{1,0:T(8,128)(2,1)S(1)} reduce(bf16[16,1,65536]{2,1,0:T(2,128)(2,1)} %reshape.147, bf16[]{:T(256)} %constant.62), dimensions={1}, to_apply=%all_to_all.5.reduce_sub_computation | reduce | bytes 4194306 | tf_op jit(solution)/shard_map/all_to_all | solution.py:26
  170.1 5.8 %reshape.124 = bf16[16,1,1,64,16,64]{5,4,3,0,2,1:T(8,128)(2,1)} reshape(bf16[16,65536]{1,0:T(8,128)(2,1)S(1)} %reduce) | data formatting | bytes 4194304 | tf_op jit(solution)/shard_map/reshape | solution.py:27
  175.9 0.0 copy-start
  175.9 5.3 %copy.30 = bf16[16,1,1,64,16,64]{5,3,0,4,1,2:T(8,128)(2,1)} copy(bf16[16,1,1,64,16,64]{5,4,3,0,2,1:T(8,128)(2,1)} %reshape.124) | data formatting | bytes 4194304 | tf_op jit(solution)/shard_map/reshape | solution.py:27
  181.1 0.0 copy-done
  181.1 5.5 %gather_fusion = bf16[256,64,64]{2,1,0:T(8,128)(2,1)} fusion(bf16[16,64,16,64]{3,1,2,0:T(8,128)(2,1)} %bitcast.88, s32[256]{0:T(256)S(1)} %copy-done), kind=kCustom, calls=%fused_computation | custom fusion | bytes 4196352 | tf_op jit(solution)/shard_map/jit(take_along_axis)/gather | solution.py:33
  186.7 7.6 %copy.29 = bf16[16,16,64,64]{3,1,2,0:T(8,128)(2,1)} copy(bf16[16,16,64,64]{3,2,1,0:T(8,128)(2,1)} %bitcast.89) | data formatting | bytes 4194304 | tf_op jit(solution)/shard_map/jit(take_along_axis)/gather | solution.py:33
  194.3 0.0 copy-start.2
  194.3 5.8 %select_n.42 = bf16[1024,1024]{1,0:T(8,128)(2,1)S(1)} reshape(bf16[16,64,16,64]{3,2,1,0:T(8,128)(2,1)} %bitcast.90) | data formatting | bytes 4194304 | tf_op jit(solution)/shard_map/jit(take_along_axis)/select_n | solution.py:33
  200.1 0.0 copy-done.2
  200.1 0.7 fusion.15
  200.8 0.7 fusion.14
  201.5 0.7 fusion.13
  202.2 0.7 fusion.12
  203.0 1.8 fusion.18
  (1 shorter events, 0.0 us)
Async XLA Ops:
  2.6 65.1 %all-to-all-start = ((bf16[16,2,256]{2,1,0:T(2,128)(2,1)}), bf16[16,2,256]{2,1,0:T(2,128)(2,1)S(1)}, u32[]{:S(2)}, u32[]{:S(2)}) async-start(bf16[16,2,256]{2,1,0:T(2,128)(2,1)} %reshape.144), calls=%async_computation | async-start | bytes 32768 | tf_op jit(solution)/shard_map/all_to_all | solution.py:21
  97.3 6.2 %copy-start.1 = (f32[16,64]{1,0:T(8,128)S(1)}, f32[16,64]{1,0:T(8,128)}, u32[]{:S(2)}) copy-start(f32[16,64]{1,0:T(8,128)} %param.9) | copy-start | bytes 12292
  97.3 53.6 %all-to-all-start.1 = ((bf16[16,2,32768]{2,1,0:T(2,128)(2,1)}), bf16[16,2,32768]{2,1,0:T(2,128)(2,1)S(1)}, u32[]{:S(2)}, u32[]{:S(2)}) async-start(bf16[16,2,32768]{2,1,0:T(2,128)(2,1)} %reshape.146), calls=%async_computation.1 | async-start | bytes 4194304 | tf_op jit(solution)/shard_map/all_to_all | solution.py:26
  175.9 5.3 %copy-start = (s32[256]{0:T(256)S(1)}, s32[256]{0:T(256)}, u32[]{:S(2)}) copy-start(s32[256]{0:T(256)} %constant.61) | copy-start | bytes 3076
  194.3 5.8 %copy-start.2 = (bf16[1,1024,256]{2,1,0:T(8,128)(2,1)S(1)}, bf16[1,1024,256]{2,1,0:T(8,128)(2,1)}, u32[]{:S(2)}) copy-start(bf16[1,1024,256]{2,1,0:T(8,128)(2,1)} %param.10) | copy-start | bytes 1572868
where the time goes:
time: 205 us
  local copies, waits for them, and re-layouts  100 us (49%)
  waiting for transfers between devices  47.3 us (23%)
  matrix products  27.4 us (13%)
  other arithmetic  16.7 us (8%)
  starting transfers between devices  12.7 us (6%)
    unnamed x12, local copies, waits for them, and re-layouts  70.4 us
    all_to_all x1, waiting for transfers between devices, per_device(): lax.all_to_all(outgoing_blocks, 'pb', split_axis=0, concat_axis=0, tiled=...  47.3 us
    dot_general x1, matrix products, per_device(): jnp.dot(arrived[:, 0, :], slab, preferred_element_type=jnp.float32)  22.8 us
    gather x2, local copies, waits for them, and re-layouts, per_device(): permuted = jnp.take_along_axis(potential, source_index, axis=3)  13.2 us
    all_to_all x1, other arithmetic, per_device(): lax.all_to_all(outgoing_blocks, 'pb', split_axis=0, concat_axis=0, tiled=...  12.4 us
    reshape x2, local copies, waits for them, and re-layouts, per_device(): relayed.reshape(kpoints, per_transfer, local_walkers, rows_here, kpoints,...  11.1 us
    all_to_all x1, starting transfers between devices, per_device(): lax.all_to_all(outgoing, 'pb', split_axis=1, concat_axis=0, tiled=True)  6.55 us
    all_to_all x1, starting transfers between devices, per_device(): lax.all_to_all(outgoing_blocks, 'pb', split_axis=0, concat_axis=0, tiled=...  6.15 us
  transfers between devices with their start and end apart: 2, of which 1 were waited for; matrix products, arithmetic and copies ran while one was open for 29% of the time, Pallas kernels for 0%

commit v1 on v0

v1 whole, which is shorter than its diff:
```python
import functools

import jax
import jax.numpy as jnp
from jax import lax
from jax.experimental import pallas as pl
from jax.experimental.pallas import tpu as pltpu
from jax.sharding import PartitionSpec as P

TERMS = 6
LANES = 128
VMEM_LIMIT = 56 * 1024 * 1024


def shift_kernel(fields_ref, shift_ref, out_ref):
    shifted = (fields_ref[...] + shift_ref[...]).astype(jnp.bfloat16).astype(jnp.float32)
    for v in range(out_ref.shape[1]):
        out_ref[:, v, :] = shifted[:, v * LANES:(v + 1) * LANES]


def shift_fields(fields, field_shift):
    kpoints, vectors = field_shift.shape
    return pl.pallas_call(
        shift_kernel,
        out_shape=jax.ShapeDtypeStruct((kpoints, vectors // LANES, LANES), jnp.float32),
    )(fields, field_shift)


def potential_kernel(shifted_ref, slab_ref, out_ref, total):
    step = pl.program_id(1)
    walkers = shifted_ref.shape[0]
    vectors, rows, columns = slab_ref.shape
    depth = vectors * rows
    spread = (
        lax.broadcasted_iota(jnp.int32, (vectors, depth), 1) // rows
        == lax.broadcasted_iota(jnp.int32, (vectors, depth), 0)
    )
    spread = jnp.where(spread, 1.0, 0.0).astype(jnp.bfloat16)
    shifted = shifted_ref[:, step, :].astype(jnp.bfloat16)
    wide = jnp.dot(shifted, spread, preferred_element_type=jnp.float32)
    same = (
        lax.broadcasted_iota(jnp.int32, (rows, depth), 1) % rows
        == lax.broadcasted_iota(jnp.int32, (rows, depth), 0)
    )
    left = jnp.concatenate(
        [
            jnp.where(same, jnp.broadcast_to(wide[w:w + 1], (rows, depth)), 0.0).astype(jnp.bfloat16)
            for w in range(walkers)
        ],
        axis=0,
    )
    part = jnp.dot(left, slab_ref[...].reshape(depth, columns), preferred_element_type=jnp.float32)

    @pl.when(step == 0)
    def _():
        total[...] = part

    @pl.when(step > 0)
    def _():
        total[...] += part

    @pl.when(step == pl.num_programs(1) - 1)
    def _():
        out_ref[...] = total[...].astype(jnp.bfloat16).reshape(out_ref.shape)


def potential_rows(shifted, slab, first, count, block_rows):
    walkers, steps, lanes = shifted.shape
    vectors, _, columns = slab.shape
    return pl.pallas_call(
        potential_kernel,
        grid=(count // block_rows, steps),
        in_specs=[
            pl.BlockSpec((walkers, steps, lanes), lambda i, g: (0, 0, 0)),
            pl.BlockSpec((lanes, block_rows, columns), lambda i, g: (g, first // block_rows + i, 0)),
        ],
        out_specs=pl.BlockSpec((walkers, block_rows, columns), lambda i, g: (0, i, 0)),
        out_shape=jax.ShapeDtypeStruct((walkers, count, columns), jnp.bfloat16),
        scratch_shapes=[pltpu.VMEM((walkers * block_rows, columns), jnp.float32)],
        compiler_params=pltpu.CompilerParams(vmem_limit_bytes=VMEM_LIMIT),
        cost_estimate=pl.CostEstimate(
            flops=2 * walkers * count * block_rows * vectors * columns,
            bytes_accessed=2 * count * vectors * columns,
            transcendentals=0,
        ),
    )(shifted, slab)


def taylor_kernel(kpoints, *refs):
    block_refs = refs[:-5]
    onebody_ref, walker_ref, out_ref, matrix, term = refs[-5:]
    size = matrix.shape[0]
    orbitals = size // kpoints
    per_tile = LANES // orbitals
    first = 0
    for block in block_refs:
        rows = block.shape[1]
        for k in range(kpoints):
            lanes = slice(k * orbitals, (k + 1) * orbitals)
            for tile in range(size // LANES):
                sources = [(k - tile * per_tile - i) % kpoints for i in range(per_tile)]
                matrix[k * orbitals + first:k * orbitals + first + rows, tile * LANES:(tile + 1) * LANES] = (
                    jnp.concatenate([block[q, :, lanes] for q in sources], axis=1)
                )
        first += rows
    term[...] = walker_ref[...]
    total = walker_ref[...].astype(jnp.float32)
    for order in range(1, TERMS):
        product = jnp.dot(matrix[...], term[...], preferred_element_type=jnp.float32)
        product = product + onebody_ref[...] * term[...].astype(jnp.float32)
        term[...] = (product * (-1.0 / order)).astype(jnp.bfloat16)
        total = total + term[...].astype(jnp.float32)
    out_ref[...] = total.astype(jnp.bfloat16)


def taylor(blocks, onebody, walker):
    kpoints, orbitals = onebody.shape
    size, columns = walker.shape
    return pl.pallas_call(
        functools.partial(taylor_kernel, kpoints),
        out_shape=jax.ShapeDtypeStruct(walker.shape, jnp.bfloat16),
        scratch_shapes=[
            pltpu.VMEM((size, size), jnp.bfloat16),
            pltpu.VMEM((size, columns), jnp.bfloat16),
        ],
        compiler_params=pltpu.CompilerParams(vmem_limit_bytes=VMEM_LIMIT),
        cost_estimate=pl.CostEstimate(
            flops=2 * (TERMS - 1) * size * size * columns,
            bytes_accessed=2 * size * (size + 2 * columns),
            transcendentals=0,
        ),
    )(*blocks, onebody.reshape(size, 1), walker)


def per_device(fields, field_shift, cholesky, onebody, walkers):
    devices = lax.axis_size("pb")
    local_walkers = fields.shape[0]
    kpoints, orbitals = onebody.shape
    vectors, rows_here, columns = cholesky.shape
    per_transfer = orbitals // rows_here
    block_rows = min(16, rows_here)
    chunks = CHUNKS if rows_here % (16 * CHUNKS) == 0 else 1

    outgoing = jnp.stack([shift_fields(fields[w], field_shift) for w in range(local_walkers)], axis=1)
    outgoing = jnp.repeat(outgoing, per_transfer, axis=0)
    arrived = lax.all_to_all(outgoing, "pb", split_axis=0, concat_axis=0, tiled=True)
    arrived = arrived.reshape((devices * local_walkers,) + arrived.shape[2:])

    count = rows_here // chunks
    relayed = []
    for chunk in range(chunks):
        blocks = potential_rows(arrived, cholesky, chunk * count, count, block_rows)
        blocks = blocks.reshape(devices, local_walkers, count, columns)
        relayed.append(lax.all_to_all(blocks, "pb", split_axis=0, concat_axis=0, tiled=True))

    results = []
    for w in range(local_walkers):
        mine = [r[:, w].reshape(kpoints, per_transfer * count, columns) for r in relayed]
        results.append(taylor(mine, onebody, walkers[w]))
    return jnp.stack(results, axis=0)


CHUNKS = 4


def solution(mesh):
    return jax.shard_map(
        per_device,
        mesh=mesh,
        in_specs=(
            P(("groups", "pb"), None, None),
            P(),
            P(None, "pb", None),
            P(),
            P(("groups", "pb"), None, None),
        ),
        out_specs=P(("groups", "pb"), None, None),
        check_vma=False,
    )
```

time: 205 us -> 108 us (0.53)
  the two profiles are of different devices: /device:TPU:15 before, /device:TPU:0 now
where the time goes in v1:
time: 108 us; the launch traced here: 107 us
  Pallas kernels  48.4 us (45%)
  waiting for transfers between devices  27 us (25%)
  starting transfers between devices  15.8 us (15%)
  blocking collectives  14.1 us (13%)
  local copies, waits for them, and re-layouts  2.11 us (2%)
    pallas_call x4, Pallas kernels, potential_rows(): pl.pallas_call(potential_kernel, grid=(count // block_rows, steps), in_sp...  39.3 us
    all_to_all x4, waiting for transfers between devices, per_device(): lax.all_to_all(blocks, 'pb', split_axis=0, concat_axis=0, tiled=True)  27 us
    all_to_all x4, starting transfers between devices, per_device(): lax.all_to_all(blocks, 'pb', split_axis=0, concat_axis=0, tiled=True)  15.8 us
    all_to_all x1, blocking collectives, per_device(): lax.all_to_all(outgoing, 'pb', split_axis=0, concat_axis=0, tiled=True)  14.1 us
    pallas_call x1, Pallas kernels, taylor(): pl.pallas_call(functools.partial(taylor_kernel, kpoints), out_shape=jax.S...  7.7 us
  transfers between devices with their start and end apart: 4, of which 4 were waited for; matrix products, arithmetic and copies ran while one was open for 1% of the time, Pallas kernels for 27%

profile of v1, /device:TPU:0, one launch (start us, length us, event | category | flops | bytes accessed | tf_op | source)
XLA Modules:
  0.0 107.5 jit_solution(14344413313008314134)
XLA Ops:
  0.0 1.4 %shard_map.55 = f32[16,4,128]{2,1,0:T(4,128)} custom-call(f32[16,512]{1,0:T(8,128)} %bitcast.36, f32[16,512]{1,0:T(8,128)} %shift_ref.1), custom_call_target="tpu_custom_call" | custom-call | tf_op jit(solution)/shard_map/pallas_call | solution.py:23
  1.4 14.1 %all_to_all.25 = f32[16,1,4,128]{3,2,1,0:T(4,128)} all-to-all(f32[16,1,4,128]{3,2,1,0:T(4,128)} %bitcast.35), channel_id=1, replica_groups=mesh['groups'=2,'pb'=16] {'pb'}, dimensions={0} | all-to-all | bytes 65536 | tf_op jit(solution)/shard_map/all_to_all | solution.py:146
  15.5 9.8 %shard_map.59 = bf16[16,16,1024]{2,1,0:T(8,128)(2,1)} custom-call(f32[16,4,128]{2,1,0:T(4,128)} %bitcast.27, bf16[512,64,1024]{2,1,0:T(8,128)(2,1)} %slab_ref.7), custom_call_target="tpu_custom_call" | custom-call | flops 4294967296 | bytes 16777216 | tf_op jit(solution)/shard_map/pallas_call | solution.py:70
  25.3 3.6 %all-to-all-start.4 = ((bf16[16,1,16,1024]{3,2,1,0:T(8,128)(2,1)}), bf16[16,1,16,1024]{3,2,1,0:T(8,128)(2,1)S(1)}, u32[]{:S(2)}, u32[]{:S(2)}) async-start(bf16[16,1,16,1024]{3,2,1,0:T(8,128)(2,1)} %bitcast.26), calls=%async_computation.4 | async-start | bytes 1048576 | tf_op jit(solution)/shard_map/all_to_all | solution.py:154
  28.9 9.8 %shard_map.58 = bf16[16,16,1024]{2,1,0:T(8,128)(2,1)} custom-call(f32[16,4,128]{2,1,0:T(4,128)} %bitcast.28, bf16[512,64,1024]{2,1,0:T(8,128)(2,1)} %slab_ref.7), custom_call_target="tpu_custom_call" | custom-call | flops 4294967296 | bytes 16777216 | tf_op jit(solution)/shard_map/pallas_call | solution.py:70
  38.7 4.6 %all-to-all-done.4 = bf16[16,1,16,1024]{3,2,1,0:T(8,128)(2,1)S(1)} async-done(((bf16[16,1,16,1024]{3,2,1,0:T(8,128)(2,1)}), bf16[16,1,16,1024]{3,2,1,0:T(8,128)(2,1)S(1)}, u32[]{:S(2)}, u32[]{:S(2)}) %all-to-all-start.4) | async-done | bytes 524320 | tf_op jit(solution)/shard_map/all_to_all | solution.py:154
  43.3 0.0 copy-start
  43.3 4.0 %all-to-all-start.3 = ((bf16[16,1,16,1024]{3,2,1,0:T(8,128)(2,1)}), bf16[16,1,16,1024]{3,2,1,0:T(8,128)(2,1)S(1)}, u32[]{:S(2)}, u32[]{:S(2)}) async-start(bf16[16,1,16,1024]{3,2,1,0:T(8,128)(2,1)} %bitcast.25), calls=%async_computation.3 | async-start | bytes 1048576 | tf_op jit(solution)/shard_map/all_to_all | solution.py:154
  47.4 0.0 copy-start.4
  47.4 9.8 %shard_map.57 = bf16[16,16,1024]{2,1,0:T(8,128)(2,1)} custom-call(f32[16,4,128]{2,1,0:T(4,128)} %bitcast.29, bf16[512,64,1024]{2,1,0:T(8,128)(2,1)} %slab_ref.7), custom_call_target="tpu_custom_call" | custom-call | flops 4294967296 | bytes 16777216 | tf_op jit(solution)/shard_map/pallas_call | solution.py:70
  57.2 4.6 %all-to-all-done.3 = bf16[16,1,16,1024]{3,2,1,0:T(8,128)(2,1)S(1)} async-done(((bf16[16,1,16,1024]{3,2,1,0:T(8,128)(2,1)}), bf16[16,1,16,1024]{3,2,1,0:T(8,128)(2,1)S(1)}, u32[]{:S(2)}, u32[]{:S(2)}) %all-to-all-start.3) | async-done | bytes 524320 | tf_op jit(solution)/shard_map/all_to_all | solution.py:154
  61.8 0.0 copy-start.1
  61.8 4.1 %all-to-all-start.2 = ((bf16[16,1,16,1024]{3,2,1,0:T(8,128)(2,1)}), bf16[16,1,16,1024]{3,2,1,0:T(8,128)(2,1)S(1)}, u32[]{:S(2)}, u32[]{:S(2)}) async-start(bf16[16,1,16,1024]{3,2,1,0:T(8,128)(2,1)} %bitcast.23), calls=%async_computation.2 | async-start | bytes 1048576 | tf_op jit(solution)/shard_map/all_to_all | solution.py:154
  65.9 9.8 %shard_map.56 = bf16[16,16,1024]{2,1,0:T(8,128)(2,1)} custom-call(f32[16,4,128]{2,1,0:T(4,128)} %bitcast.30, bf16[512,64,1024]{2,1,0:T(8,128)(2,1)} %slab_ref.7), custom_call_target="tpu_custom_call" | custom-call | flops 4294967296 | bytes 16777216 | tf_op jit(solution)/shard_map/pallas_call | solution.py:70
  75.8 0.0 copy-done
  75.8 4.6 %all-to-all-done.2 = bf16[16,1,16,1024]{3,2,1,0:T(8,128)(2,1)S(1)} async-done(((bf16[16,1,16,1024]{3,2,1,0:T(8,128)(2,1)}), bf16[16,1,16,1024]{3,2,1,0:T(8,128)(2,1)S(1)}, u32[]{:S(2)}, u32[]{:S(2)}) %all-to-all-start.2) | async-done | bytes 524320 | tf_op jit(solution)/shard_map/all_to_all | solution.py:154
  80.4 0.0 copy-start.2
  80.4 4.1 %all-to-all-start.1 = ((bf16[16,1,16,1024]{3,2,1,0:T(8,128)(2,1)}), bf16[16,1,16,1024]{3,2,1,0:T(8,128)(2,1)S(1)}, u32[]{:S(2)}, u32[]{:S(2)}) async-start(bf16[16,1,16,1024]{3,2,1,0:T(8,128)(2,1)} %bitcast.24), calls=%async_computation.1 | async-start | bytes 1048576 | tf_op jit(solution)/shard_map/all_to_all | solution.py:154
  84.5 0.0 copy-done.4
  84.5 1.3 %reshape.24.refs_4_ = f32[1024,1]{1,0:T(8,128)} reshape(f32[16,64]{1,0:T(8,128)S(1)} %copy-done.4) | data formatting | bytes 8192 | tf_op jit(solution)/shard_map/reshape | solution.py:132
  85.8 13.2 %all-to-all-done.1 = bf16[16,1,16,1024]{3,2,1,0:T(8,128)(2,1)S(1)} async-done(((bf16[16,1,16,1024]{3,2,1,0:T(8,128)(2,1)}), bf16[16,1,16,1024]{3,2,1,0:T(8,128)(2,1)S(1)}, u32[]{:S(2)}, u32[]{:S(2)}) %all-to-all-start.1) | async-done | bytes 524320 | tf_op jit(solution)/shard_map/all_to_all | solution.py:154
  99.0 0.0 copy-start.3
  99.0 0.0 copy-done.1
  99.0 0.0 copy-done.2
  99.0 0.8 copy-done.3
  99.8 7.7 %shard_map.60 = bf16[1024,256]{1,0:T(8,128)(2,1)} custom-call(bf16[16,16,1024]{2,1,0:T(8,128)(2,1)} %bitcast.34, bf16[16,16,1024]{2,1,0:T(8,128)(2,1)} %bitcast.33, bf16[16,16,1024]{2,1,0:T(8,128)(2,1)} %bitcast.32, bf16[16,16,1024]{2,1,0:T(8,128)(2,1)} %bitcast.31, f32[1024,1]{1,0:T(8,128)} %reshape.24.refs_4_, bf16[1024,256]{1,0:T(8,128)(2,1)} %bitcast.37), custom_call_target="tpu_custom_call" | custom-call | flops 2684354560 | bytes 3145728 | tf_op jit(solution)/shard_map/pallas_call | solution.py:119
Async XLA Ops:
  25.3 18.0 %all-to-all-start.4 = ((bf16[16,1,16,1024]{3,2,1,0:T(8,128)(2,1)}), bf16[16,1,16,1024]{3,2,1,0:T(8,128)(2,1)S(1)}, u32[]{:S(2)}, u32[]{:S(2)}) async-start(bf16[16,1,16,1024]{3,2,1,0:T(8,128)(2,1)} %bitcast.26), calls=%async_computation.4 | async-start | bytes 1048576 | tf_op jit(solution)/shard_map/all_to_all | solution.py:154
  43.3 32.4 %copy-start = (bf16[16,1,16,1024]{3,2,1,0:T(8,128)(2,1)}, bf16[16,1,16,1024]{3,2,1,0:T(8,128)(2,1)S(1)}, u32[]{:S(2)}) copy-start(bf16[16,1,16,1024]{3,2,1,0:T(8,128)(2,1)S(1)} %all-to-all-done.4) | copy-start | bytes 1572868
  43.3 18.5 %all-to-all-start.3 = ((bf16[16,1,16,1024]{3,2,1,0:T(8,128)(2,1)}), bf16[16,1,16,1024]{3,2,1,0:T(8,128)(2,1)S(1)}, u32[]{:S(2)}, u32[]{:S(2)}) async-start(bf16[16,1,16,1024]{3,2,1,0:T(8,128)(2,1)} %bitcast.25), calls=%async_computation.3 | async-start | bytes 1048576 | tf_op jit(solution)/shard_map/all_to_all | solution.py:154
  47.4 37.2 %copy-start.4 = (f32[16,64]{1,0:T(8,128)S(1)}, f32[16,64]{1,0:T(8,128)}, u32[]{:S(2)}) copy-start(f32[16,64]{1,0:T(8,128)} %param.8) | copy-start | bytes 12292
  61.8 37.2 %copy-start.1 = (bf16[16,1,16,1024]{3,2,1,0:T(8,128)(2,1)}, bf16[16,1,16,1024]{3,2,1,0:T(8,128)(2,1)S(1)}, u32[]{:S(2)}) copy-start(bf16[16,1,16,1024]{3,2,1,0:T(8,128)(2,1)S(1)} %all-to-all-done.3) | copy-start | bytes 1572868
  61.8 18.6 %all-to-all-start.2 = ((bf16[16,1,16,1024]{3,2,1,0:T(8,128)(2,1)}), bf16[16,1,16,1024]{3,2,1,0:T(8,128)(2,1)S(1)}, u32[]{:S(2)}, u32[]{:S(2)}) async-start(bf16[16,1,16,1024]{3,2,1,0:T(8,128)(2,1)} %bitcast.23), calls=%async_computation.2 | async-start | bytes 1048576 | tf_op jit(solution)/shard_map/all_to_all | solution.py:154
  80.4 18.6 %copy-start.2 = (bf16[16,1,16,1024]{3,2,1,0:T(8,128)(2,1)}, bf16[16,1,16,1024]{3,2,1,0:T(8,128)(2,1)S(1)}, u32[]{:S(2)}) copy-start(bf16[16,1,16,1024]{3,2,1,0:T(8,128)(2,1)S(1)} %all-to-all-done.2) | copy-start | bytes 1572868
  80.4 18.6 %all-to-all-start.1 = ((bf16[16,1,16,1024]{3,2,1,0:T(8,128)(2,1)}), bf16[16,1,16,1024]{3,2,1,0:T(8,128)(2,1)S(1)}, u32[]{:S(2)}, u32[]{:S(2)}) async-start(bf16[16,1,16,1024]{3,2,1,0:T(8,128)(2,1)} %bitcast.24), calls=%async_computation.1 | async-start | bytes 1048576 | tf_op jit(solution)/shard_map/all_to_all | solution.py:154
  99.0 0.8 copy-start.3

commit v2 on v0

v2 whole, which is shorter than its diff:
```python
import functools

import jax
import jax.numpy as jnp
from jax import lax
from jax.experimental import pallas as pl
from jax.experimental.pallas import tpu as pltpu
from jax.sharding import PartitionSpec as P

TERMS = 6
LANES = 128
STRIP = 8
PART = 128
VMEM_LIMIT = 56 * 1024 * 1024
MIDDLE_VMEM_LIMIT = 24 * 1024 * 1024
SMALL_VMEM_LIMIT = 8 * 1024 * 1024


def shift_kernel(fields_ref, shift_ref, out_ref):
    shifted = (fields_ref[...] + shift_ref[...]).astype(jnp.bfloat16).astype(jnp.float32)
    for v in range(out_ref.shape[1]):
        out_ref[:, v, :] = shifted[:, v * LANES:(v + 1) * LANES]


def shift_fields(fields, field_shift):
    kpoints, vectors = field_shift.shape
    return pl.pallas_call(
        shift_kernel,
        out_shape=jax.ShapeDtypeStruct((kpoints, vectors // LANES, LANES), jnp.float32),
    )(fields, field_shift)


def potential_kernel(plan, shifted_ref, slab_ref, *refs):
    offset, count, far, own, devices = plan
    far_refs, all_ref, (slab, left, total, arrived) = refs[:far], refs[far], refs[far + 1:]
    walkers, blocks, _ = shifted_ref.shape
    vectors, _, columns = slab.shape
    parts = vectors // PART
    height = min(16, count)
    me, group = lax.axis_index("pb"), lax.axis_index("groups")
    first = offset if own == slab_ref.shape[1] else pl.multiple_of(group * own + offset, height)

    def fetch(block, part):
        return pltpu.make_async_copy(
            slab_ref.at[pl.ds(part * PART, PART), pl.ds(first + block * height, height)],
            slab.at[pl.ds(part * PART, PART), pl.ds(block * height, height)],
            arrived.at[block, part],
        )

    for block in range(count // height):
        for part in range(parts):
            fetch(block, part).start()

    depth = LANES * STRIP
    spread = (
        lax.broadcasted_iota(jnp.int32, (LANES, depth), 1) // STRIP
        == lax.broadcasted_iota(jnp.int32, (LANES, depth), 0)
    )
    spread = jnp.where(spread, 1.0, 0.0).astype(jnp.bfloat16)
    same = (
        lax.broadcasted_iota(jnp.int32, (STRIP, depth), 1) % STRIP
        == lax.broadcasted_iota(jnp.int32, (STRIP, depth), 0)
    )
    order = far_places(far, devices, group, me) + near_places(walkers - far, devices, me)
    rows_of = [shifted_ref[g * devices + d] for g, d in order]
    for v in range(blocks):
        shifted = jnp.concatenate([row[v:v + 1] for row in rows_of], axis=0).astype(jnp.bfloat16)
        wide = jnp.dot(shifted, spread, preferred_element_type=jnp.float32)
        for pair in range(walkers // 2):
            left[pair * 16:pair * 16 + 16, v * depth:(v + 1) * depth] = jnp.concatenate(
                [
                    jnp.where(same, jnp.broadcast_to(wide[w:w + 1], (STRIP, depth)), 0.0)
                    for w in (2 * pair, 2 * pair + 1)
                ],
                axis=0,
            ).astype(jnp.bfloat16)

    strips = height // STRIP
    for block in range(count // height):
        for part in range(parts):
            fetch(block, part).wait()
            for strip in range(strips):
                top = block * height + strip * STRIP
                product = jnp.dot(
                    left[:, part * PART * STRIP:(part + 1) * PART * STRIP],
                    slab[part * PART:(part + 1) * PART, top:top + STRIP].reshape(PART * STRIP, columns),
                    preferred_element_type=jnp.float32,
                )
                if part == 0:
                    total[strip] = product
                else:
                    total[strip] += product
        for i in range(walkers):
            value = jnp.concatenate(
                [total[strip, i * STRIP:(i + 1) * STRIP] for strip in range(strips)], axis=0
            ).astype(jnp.bfloat16)
            if i < far:
                far_refs[i][block * height:(block + 1) * height] = value
            else:
                all_ref[i - far, block * height:(block + 1) * height] = value


def far_places(far, devices, group, me):
    half = devices // 2
    return [(group ^ (i // half), me ^ (half + i % half)) for i in range(far)]


def near_places(count, devices, me):
    half = devices // 2
    if count % devices:
        return [(j // half, me // half * half + j % half) for j in range(count)]
    if count >= 2 * devices or count == devices:
        return [(j // devices, j % devices) for j in range(count)]


def potential_rows(shifted, slab, plan):
    offset, count, far, own, devices = plan
    walkers, blocks, _ = shifted.shape
    vectors, _, columns = slab.shape
    height = min(16, count)
    return pl.pallas_call(
        functools.partial(potential_kernel, plan),
        in_specs=[pl.BlockSpec(memory_space=pltpu.VMEM), pl.BlockSpec(memory_space=pl.ANY)],
        out_shape=[jax.ShapeDtypeStruct((count, columns), jnp.bfloat16) for _ in range(far)]
        + [jax.ShapeDtypeStruct((walkers - far, count, columns), jnp.bfloat16)],
        scratch_shapes=[
            pltpu.VMEM((vectors, count, columns), slab.dtype),
            pltpu.VMEM((walkers * STRIP, vectors * STRIP), jnp.bfloat16),
            pltpu.VMEM((height // STRIP, walkers * STRIP, columns), jnp.float32),
            pltpu.SemaphoreType.DMA((count // height, vectors // PART)),
        ],
        compiler_params=pltpu.CompilerParams(vmem_limit_bytes=VMEM_LIMIT),
        cost_estimate=pl.CostEstimate(
            flops=2 * walkers * STRIP * count * vectors * columns,
            bytes_accessed=2 * count * vectors * columns,
            transcendentals=0,
        ),
    )(shifted, slab)


def stage(inputs, potential, arrived):
    kpoints, shares, _, _ = potential.shape
    far = len(inputs) - 1
    me, group = lax.axis_index("pb"), lax.axis_index("groups")
    copies = [(inputs[i], potential.at[d, g]) for i, (g, d) in enumerate(far_places(far, kpoints, group, me))]
    each = inputs[far].shape[0] // shares
    base = me // each * each if far else 0
    copies += [
        (inputs[far].at[pl.ds(s * each, each)], potential.at[pl.ds(base, each), s]) for s in range(shares)
    ]
    copies = [pltpu.make_async_copy(a, b, arrived.at[n]) for n, (a, b) in enumerate(copies)]
    for copy in copies:
        copy.start()
    for copy in copies:
        copy.wait()


def arrange(potential, matrix):
    kpoints, shares, rows, size = potential.shape
    orbitals = size // kpoints
    per_tile = LANES // orbitals
    for k in range(kpoints):
        lanes = slice(k * orbitals, (k + 1) * orbitals)
        for tile in range(kpoints // per_tile):
            sources = [(k - tile * per_tile - i) % kpoints for i in range(per_tile)]
            for s in range(shares):
                top = (k * shares + s) * rows
                matrix[top:top + rows, tile * LANES:(tile + 1) * LANES] = jnp.concatenate(
                    [potential[q, s, :, lanes] for q in sources], axis=1
                )


def first_kernel(count, *refs):
    inputs, (walker_ref, matrix, product, potential, arrived) = refs[:count], refs[count:]
    stage(inputs, potential, arrived)
    arrange(potential, matrix)
    product[...] = jnp.dot(matrix[...], walker_ref[...], preferred_element_type=jnp.float32)


def first_rows(inputs, shares, kpoints, walker):
    size, columns = walker.shape
    rows = inputs[-1].shape[1]
    return pl.pallas_call(
        functools.partial(first_kernel, len(inputs)),
        in_specs=[pl.BlockSpec(memory_space=pl.ANY)] * len(inputs) + [pl.BlockSpec(memory_space=pltpu.VMEM)],
        out_shape=[
            jax.ShapeDtypeStruct((kpoints * shares * rows, size), jnp.bfloat16),
            jax.ShapeDtypeStruct((kpoints * shares * rows, columns), jnp.float32),
        ],
        scratch_shapes=[
            pltpu.VMEM((kpoints, shares, rows, size), jnp.bfloat16),
            pltpu.SemaphoreType.DMA((len(inputs) - 1 + shares,)),
        ],
        compiler_params=pltpu.CompilerParams(vmem_limit_bytes=SMALL_VMEM_LIMIT),
        cost_estimate=pl.CostEstimate(
            flops=2 * kpoints * shares * rows * size * columns,
            bytes_accessed=4 * kpoints * shares * rows * size,
            transcendentals=0,
        ),
    )(*inputs, walker)


def taylor_kernel(chunks, count, *refs):
    done = len(chunks) - 1
    inputs, refs = refs[:count], refs[count:]
    sources, refs = refs[:2 * done], refs[2 * done:]
    held, refs = refs[len(refs) - 2 * done:], refs[:len(refs) - 2 * done]
    onebody_ref, walker_ref, out_ref, potential, matrix, term, total, arrived, done_arrived = refs
    kpoints, shares, _, _ = potential.shape
    own = term.shape[1] // shares
    columns = walker_ref.shape[1]
    copies = [pltpu.make_async_copy(a, b, done_arrived.at[n]) for n, (a, b) in enumerate(zip(sources, held))]
    for copy in copies:
        copy.start()
    stage(inputs, potential, arrived)
    arrange(potential, matrix)
    term[...] = walker_ref[...].reshape(term.shape)
    total[...] = term[...].astype(jnp.float32)
    for copy in copies:
        copy.wait()
    matrices = list(held[::2]) + [matrix]
    for order in range(1, TERMS):
        now = term[...].reshape(walker_ref.shape)
        new = [
            held[2 * i + 1][...] if order == 1 and i < done
            else jnp.dot(m[...], now, preferred_element_type=jnp.float32)
            for i, m in enumerate(matrices)
        ]
        for (first, rows), product in zip(chunks, new):
            product = product.reshape(kpoints, shares, rows, columns)
            for s in range(shares):
                here = slice(s * own + first, s * own + first + rows)
                value = product[:, s] + onebody_ref[:, here] * term[:, here].astype(jnp.float32)
                value = (value * (-1.0 / order)).astype(jnp.bfloat16)
                term[:, here] = value
                total[:, here] += value.astype(jnp.float32)
    out_ref[...] = total[...].astype(jnp.bfloat16).reshape(out_ref.shape)


def taylor(inputs, shares, chunks, done, onebody, walker):
    kpoints, orbitals = onebody.shape
    size, columns = walker.shape
    rows = inputs[-1].shape[1]
    whole, anywhere = pl.BlockSpec(memory_space=pltpu.VMEM), pl.BlockSpec(memory_space=pl.ANY)
    parts = [part for pair in done for part in pair]
    return pl.pallas_call(
        functools.partial(taylor_kernel, chunks, len(inputs)),
        in_specs=[anywhere] * (len(inputs) + len(parts)) + [whole] * 2,
        out_shape=jax.ShapeDtypeStruct(walker.shape, jnp.bfloat16),
        scratch_shapes=[
            pltpu.VMEM((kpoints, shares, rows, size), jnp.bfloat16),
            pltpu.VMEM((kpoints * shares * rows, size), jnp.bfloat16),
            pltpu.VMEM((kpoints, orbitals, columns), jnp.bfloat16),
            pltpu.VMEM((kpoints, orbitals, columns), jnp.float32),
            pltpu.SemaphoreType.DMA((len(inputs) - 1 + shares,)),
            pltpu.SemaphoreType.DMA((max(len(parts), 1),)),
        ]
        + [pltpu.VMEM(part.shape, part.dtype) for part in parts],
        compiler_params=pltpu.CompilerParams(vmem_limit_bytes=MIDDLE_VMEM_LIMIT),
        cost_estimate=pl.CostEstimate(
            flops=2 * (TERMS - 1) * size * size * columns,
            bytes_accessed=2 * size * (size + 2 * columns),
            transcendentals=0,
        ),
    )(*inputs, *parts, onebody.reshape(kpoints, orbitals, 1), walker)


def exchange(blocks, axes):
    return lax.all_to_all(blocks, axes, split_axis=0, concat_axis=0, tiled=True)


def per_device(fields, field_shift, cholesky, onebody, walkers):
    devices, groups = lax.axis_size("pb"), lax.axis_size("groups")
    local_walkers = fields.shape[0]
    kpoints, orbitals = onebody.shape
    vectors, rows_here, columns = cholesky.shape
    per_transfer = orbitals // rows_here

    shares = groups if local_walkers == 1 and per_transfer == 1 and rows_here % (16 * groups) == 0 else 1
    axes = ("groups", "pb") if shares > 1 else "pb"
    outgoing = jnp.stack([shift_fields(fields[w], field_shift) for w in range(local_walkers)], axis=1)
    outgoing = jnp.tile(jnp.repeat(outgoing, per_transfer, axis=0), (shares, 1, 1, 1))
    arrived = exchange(outgoing, axes)
    arrived = arrived.reshape((shares * devices * local_walkers,) + arrived.shape[2:])

    own = rows_here // shares
    if shares > 1:
        (blocks,) = potential_rows(arrived, cholesky, (0, own, 0, own, devices))
        return taylor([exchange(blocks, axes)], shares, [(0, own)], [], onebody, walkers[0])[None]

    (blocks,) = potential_rows(arrived, cholesky, (0, own, 0, own, devices))
    relayed = exchange(blocks.reshape(devices, local_walkers, rows_here, columns), axes)
    results = [
        taylor(
            [relayed[:, w].reshape(kpoints, orbitals, columns)], 1, [(0, orbitals)], [], onebody, walkers[w]
        )
        for w in range(local_walkers)
    ]
    return jnp.stack(results, axis=0)


def solution(mesh):
    return jax.shard_map(
        per_device,
        mesh=mesh,
        in_specs=(
            P(("groups", "pb"), None, None),
            P(),
            P(None, "pb", None),
            P(),
            P(("groups", "pb"), None, None),
        ),
        out_specs=P(("groups", "pb"), None, None),
        check_vma=False,
    )
```

time: 205 us -> 90.2 us (0.44)
  the two profiles are of different devices: /device:TPU:15 before, /device:TPU:0 now
where the time goes in v2:
time: 90.2 us; the launch traced here: 89.8 us
  waiting for transfers between devices  49.5 us (55%)
  Pallas kernels  21.8 us (24%)
  blocking collectives  14.6 us (16%)
  starting transfers between devices  2.87 us (3%)
  local copies, waits for them, and re-layouts  1.02 us (1%)
    all_to_all x1, waiting for transfers between devices, exchange(): return lax.all_to_all(blocks, axes, split_axis=0, concat_axis=0, tiled=True)  49.5 us
    all_to_all x1, blocking collectives, exchange(): return lax.all_to_all(blocks, axes, split_axis=0, concat_axis=0, tiled=True)  14.6 us
    pallas_call x1, Pallas kernels, potential_rows(): pl.pallas_call(functools.partial(potential_kernel, plan), in_specs=[pl.Bl...  14.2 us
    pallas_call x1, Pallas kernels, taylor(): pl.pallas_call(functools.partial(taylor_kernel, chunks, len(inputs)), in_...  6.12 us
    all_to_all x1, starting transfers between devices, exchange(): return lax.all_to_all(blocks, axes, split_axis=0, concat_axis=0, tiled=True)  2.87 us
  transfers between devices with their start and end apart: 1, of which 1 were waited for; matrix products, arithmetic and copies ran while one was open for 0% of the time, Pallas kernels for 0%

profile of v2, /device:TPU:0, one launch (start us, length us, event | category | flops | bytes accessed | tf_op | source)
XLA Modules:
  0.0 89.8 jit_solution(6109878300973367816)
XLA Ops:
  0.0 1.4 %shard_map.55 = f32[16,4,128]{2,1,0:T(4,128)} custom-call(f32[16,512]{1,0:T(8,128)} %bitcast.9, f32[16,512]{1,0:T(8,128)} %shift_ref.1), custom_call_target="tpu_custom_call" | custom-call | tf_op jit(solution)/shard_map/pallas_call | solution.py:27
  1.4 0.8 tile.8
  2.2 14.6 %all_to_all.10 = f32[32,1,4,128]{3,2,1,0:T(4,128)} all-to-all(f32[32,1,4,128]{3,2,1,0:T(4,128)S(1)} %bitcast.8), channel_id=1, replica_groups=mesh['groups'=2,'pb'=16] {'groups','pb'}, dimensions={0} | all-to-all | bytes 131072 | tf_op jit(solution)/shard_map/all_to_all | solution.py:269
  16.8 14.2 %shard_map.56 = bf16[32,32,1024]{2,1,0:T(8,128)(2,1)} custom-call(f32[32,4,128]{2,1,0:T(4,128)} %bitcast.7, bf16[512,64,1024]{2,1,0:T(8,128)(2,1)} %slab_ref.1), custom_call_target="tpu_custom_call" | custom-call | flops 8589934592 | bytes 33554432 | tf_op jit(solution)/shard_map/pallas_call | solution.py:121
  31.1 0.0 copy-start.1
  31.1 0.0 copy-start
  31.1 2.9 %all-to-all-start.1 = ((bf16[32,32,1024]{2,1,0:T(8,128)(2,1)}), bf16[32,32,1024]{2,1,0:T(8,128)(2,1)S(1)}, u32[]{:S(2)}, u32[]{:S(2)}) async-start(bf16[32,32,1024]{2,1,0:T(8,128)(2,1)} %shard_map.56), calls=%async_computation.1 | async-start | bytes 4194304 | tf_op jit(solution)/shard_map/all_to_all | solution.py:269
  34.0 0.0 copy-done.1
  34.0 0.2 copy.7.refs_1_
  34.2 49.5 %all-to-all-done.1.refs_0_ = bf16[32,32,1024]{2,1,0:T(8,128)(2,1)S(1)} async-done(((bf16[32,32,1024]{2,1,0:T(8,128)(2,1)}), bf16[32,32,1024]{2,1,0:T(8,128)(2,1)S(1)}, u32[]{:S(2)}, u32[]{:S(2)}) %all-to-all-start.1) | async-done | bytes 2097184 | tf_op jit(solution)/shard_map/all_to_all | solution.py:269
  83.7 0.0 copy-done
  83.7 6.1 %shard_map.57 = bf16[1024,256]{1,0:T(8,128)(2,1)} custom-call(bf16[32,32,1024]{2,1,0:T(8,128)(2,1)S(1)} %all-to-all-done.1.refs_0_, f32[16,64,1]{2,1,0:T(8,128)S(1)} %copy.7.refs_1_, bf16[1024,256]{1,0:T(8,128)(2,1)S(1)} %bitcast.6), custom_call_target="tpu_custom_call" | custom-call | flops 2684354560 | bytes 3145728 | tf_op jit(solution)/shard_map/pallas_call | solution.py:246
Async XLA Ops:
  31.1 2.9 %copy-start.1 = (f32[16,64]{1,0:T(8,128)S(1)}, f32[16,64]{1,0:T(8,128)}, u32[]{:S(2)}) copy-start(f32[16,64]{1,0:T(8,128)} %param.8) | copy-start | bytes 12292
  31.1 52.6 %copy-start = (bf16[1,1024,256]{2,1,0:T(8,128)(2,1)S(1)}, bf16[1,1024,256]{2,1,0:T(8,128)(2,1)}, u32[]{:S(2)}) copy-start(bf16[1,1024,256]{2,1,0:T(8,128)(2,1)} %param.9) | copy-start | bytes 1572868
  31.1 52.6 %all-to-all-start.1 = ((bf16[32,32,1024]{2,1,0:T(8,128)(2,1)}), bf16[32,32,1024]{2,1,0:T(8,128)(2,1)S(1)}, u32[]{:S(2)}, u32[]{:S(2)}) async-start(bf16[32,32,1024]{2,1,0:T(8,128)(2,1)} %shard_map.56), calls=%async_computation.1 | async-start | bytes 4194304 | tf_op jit(solution)/shard_map/all_to_all | solution.py:269

commit v3 on v0

v3 whole, which is shorter than its diff:
```python
import jax
import jax.numpy as jnp
from jax import lax
from jax.experimental import pallas as pl
from jax.experimental.pallas import tpu as pltpu
from jax.sharding import PartitionSpec as P

TERMS = 6
LANES = 128
STRIP = 8
PART = 128
BAND = 4
MIB = 1024 * 1024


def shift_kernel(fields_ref, shift_ref, out_ref, fields, shift, arrived):
    copies = [
        pltpu.make_async_copy(fields_ref, fields, arrived.at[0]),
        pltpu.make_async_copy(shift_ref, shift, arrived.at[1]),
    ]
    for copy in copies:
        copy.start()
    for copy in copies:
        copy.wait()
    shifted = (fields[...] + shift[...]).astype(jnp.bfloat16).astype(jnp.float32)
    for copy in range(out_ref.shape[0]):
        for v in range(out_ref.shape[2]):
            out_ref[copy, :, v, :] = shifted[:, v * LANES:(v + 1) * LANES]


def shift_fields(fields, field_shift, copies):
    kpoints, vectors = field_shift.shape
    return pl.pallas_call(
        shift_kernel,
        in_specs=[pl.BlockSpec(memory_space=pl.ANY)] * 2,
        out_shape=jax.ShapeDtypeStruct((copies, kpoints, vectors // LANES, LANES), jnp.float32),
        scratch_shapes=[
            pltpu.VMEM(fields.shape, jnp.float32),
            pltpu.VMEM(field_shift.shape, jnp.float32),
            pltpu.SemaphoreType.DMA((2,)),
        ],
        compiler_params=pltpu.CompilerParams(vmem_limit_bytes=8 * MIB),
    )(fields, field_shift)


def potential_kernel(shifted_ref, slab_ref, out_ref, slab, left, total, arrived):
    walkers, blocks, _ = shifted_ref.shape
    vectors, rows, columns = slab.shape
    row_blocks, parts = arrived.shape
    height = rows // row_blocks
    strips = height // STRIP
    whole = rows == slab_ref.shape[1]
    first = 0 if whole else pl.multiple_of(lax.axis_index("groups") * rows, rows)

    def fetch(block, part):
        return pltpu.make_async_copy(
            slab_ref.at[pl.ds(part * PART, PART), pl.ds(first + block * height, height)],
            slab.at[pl.ds(part * PART, PART), pl.ds(block * height, height)],
            arrived.at[block, part],
        )

    for block in range(row_blocks):
        for part in range(parts):
            fetch(block, part).start()

    depth = LANES * STRIP
    spread = (
        lax.broadcasted_iota(jnp.int32, (LANES, depth), 1) // STRIP
        == lax.broadcasted_iota(jnp.int32, (LANES, depth), 0)
    )
    spread = jnp.where(spread, 1.0, 0.0).astype(jnp.bfloat16)
    same = (
        lax.broadcasted_iota(jnp.int32, (STRIP, depth), 1) % STRIP
        == lax.broadcasted_iota(jnp.int32, (STRIP, depth), 0)
    )
    for v in range(blocks):
        shifted = shifted_ref[:, v, :].astype(jnp.bfloat16)
        wide = jnp.dot(shifted, spread, preferred_element_type=jnp.float32)
        for pair in range(walkers // 2):
            left[pair * 16:pair * 16 + 16, v * depth:(v + 1) * depth] = jnp.concatenate(
                [
                    jnp.where(same, jnp.broadcast_to(wide[w:w + 1], (STRIP, depth)), 0.0)
                    for w in (2 * pair, 2 * pair + 1)
                ],
                axis=0,
            ).astype(jnp.bfloat16)

    for block in range(row_blocks):
        for part in range(parts):
            fetch(block, part).wait()
            for strip in range(strips):
                top = block * height + strip * STRIP
                product = jnp.dot(
                    left[:, part * PART * STRIP:(part + 1) * PART * STRIP],
                    slab[part * PART:(part + 1) * PART, top:top + STRIP].reshape(PART * STRIP, columns),
                    preferred_element_type=jnp.float32,
                )
                if part == 0:
                    total[strip] = product
                else:
                    total[strip] += product
        for w in range(walkers):
            out_ref[w, block * height:(block + 1) * height] = jnp.concatenate(
                [total[strip, w * STRIP:(w + 1) * STRIP] for strip in range(strips)], axis=0
            ).astype(jnp.bfloat16)


def potential_rows(shifted, slab, rows):
    walkers, blocks, _ = shifted.shape
    vectors, _, columns = slab.shape
    height = min(16, rows)
    scratch = 2 * vectors * rows * columns + 2 * walkers * STRIP * (vectors * STRIP + 2 * (height // STRIP) * columns)
    return pl.pallas_call(
        potential_kernel,
        in_specs=[pl.BlockSpec(memory_space=pltpu.VMEM), pl.BlockSpec(memory_space=pl.ANY)],
        out_shape=jax.ShapeDtypeStruct((walkers, rows, columns), jnp.bfloat16),
        scratch_shapes=[
            pltpu.VMEM((vectors, rows, columns), slab.dtype),
            pltpu.VMEM((walkers * STRIP, vectors * STRIP), jnp.bfloat16),
            pltpu.VMEM((height // STRIP, walkers * STRIP, columns), jnp.float32),
            pltpu.SemaphoreType.DMA((rows // height, vectors // PART)),
        ],
        compiler_params=pltpu.CompilerParams(vmem_limit_bytes=scratch + 10 * MIB),
        cost_estimate=pl.CostEstimate(
            flops=2 * walkers * STRIP * rows * vectors * columns,
            bytes_accessed=2 * rows * vectors * columns,
            transcendentals=0,
        ),
    )(shifted, slab)


def taylor_kernel(blocks_ref, onebody_ref, walker_ref, out_ref, matrix, diagonal, terms):
    shares, kpoints, rows, size = blocks_ref.shape
    orbitals = size // kpoints
    columns = walker_ref.shape[1]
    per_tile = LANES // orbitals
    for k in range(kpoints):
        lanes = slice(k * orbitals, (k + 1) * orbitals)
        for tile in range(kpoints // per_tile):
            sources = [(k - tile * per_tile - i) % kpoints for i in range(per_tile)]
            for s in range(shares):
                top = k * orbitals + s * rows
                matrix[top:top + rows, tile * LANES:(tile + 1) * LANES] = jnp.concatenate(
                    [blocks_ref[s, q, :, lanes] for q in sources], axis=1
                )
    diagonal[...] = jnp.broadcast_to(onebody_ref[...], diagonal.shape)
    for order in range(1, TERMS):
        before = walker_ref if order == 1 else terms.at[order - 2]
        for first in range(0, kpoints, BAND):
            band = slice(first * orbitals, (first + BAND) * orbitals)
            product = jnp.dot(matrix[band], before[...], preferred_element_type=jnp.float32)
            here = before[band].astype(jnp.float32)
            product += jnp.concatenate([diagonal[band]] * (columns // LANES), axis=1) * here
            value = (product * (-1.0 / order)).astype(jnp.bfloat16)
            if order < TERMS - 1:
                terms[order - 1, band] = value
            else:
                total = walker_ref[band].astype(jnp.float32)
                for n in range(TERMS - 2):
                    total += terms[n, band].astype(jnp.float32)
                out_ref[band] = (total + value.astype(jnp.float32)).astype(jnp.bfloat16)


def taylor(blocks, onebody, walker):
    kpoints, orbitals = onebody.shape
    size, columns = walker.shape
    return pl.pallas_call(
        taylor_kernel,
        out_shape=jax.ShapeDtypeStruct(walker.shape, jnp.bfloat16),
        scratch_shapes=[
            pltpu.VMEM((size, size), jnp.bfloat16),
            pltpu.VMEM((size, LANES), jnp.float32),
            pltpu.VMEM((TERMS - 2, size, columns), jnp.bfloat16),
        ],
        compiler_params=pltpu.CompilerParams(vmem_limit_bytes=24 * MIB),
        cost_estimate=pl.CostEstimate(
            flops=2 * (TERMS - 1) * size * size * columns,
            bytes_accessed=2 * size * (size + 2 * columns),
            transcendentals=0,
        ),
    )(blocks, onebody.reshape(size, 1), walker)


def exchange(blocks, axes):
    return lax.all_to_all(blocks, axes, split_axis=0, concat_axis=0, tiled=True)


def per_device(fields, field_shift, cholesky, onebody, walkers):
    devices, groups = lax.axis_size("pb"), lax.axis_size("groups")
    local_walkers = fields.shape[0]
    kpoints, orbitals = onebody.shape
    vectors, rows_here, columns = cholesky.shape
    per_transfer = orbitals // rows_here

    shares = groups if local_walkers == 1 and per_transfer == 1 and rows_here % (16 * groups) == 0 else 1
    axes = ("groups", "pb") if shares > 1 else "pb"
    rows = rows_here // shares
    outgoing = [shift_fields(fields[w], field_shift, shares) for w in range(local_walkers)]
    outgoing = jnp.repeat(jnp.stack(outgoing, axis=2), per_transfer, axis=1)
    arrived = exchange(outgoing.reshape((shares * devices,) + outgoing.shape[2:]), axes)
    arrived = arrived.reshape((shares * devices * local_walkers,) + arrived.shape[2:])

    blocks = potential_rows(arrived, cholesky, rows)
    relayed = exchange(blocks.reshape(shares * devices, local_walkers, rows, columns), axes)
    results = [
        taylor(relayed[:, w].reshape(shares, kpoints, per_transfer * rows, columns), onebody, walkers[w])
        for w in range(local_walkers)
    ]
    return jnp.stack(results, axis=0)


def solution(mesh):
    return jax.shard_map(
        per_device,
        mesh=mesh,
        in_specs=(
            P(("groups", "pb"), None, None),
            P(),
            P(None, "pb", None),
            P(),
            P(("groups", "pb"), None, None),
        ),
        out_specs=P(("groups", "pb"), None, None),
        check_vma=False,
    )
```

time: 205 us -> 87 us (0.42)
  the two profiles are of different devices: /device:TPU:15 before, /device:TPU:0 now
where the time goes in v3:
time: 87 us; the launch traced here: 86.7 us
  waiting for transfers between devices  49.2 us (57%)
  Pallas kernels  18 us (21%)
  blocking collectives  14.5 us (17%)
  starting transfers between devices  2.87 us (3%)
  local copies, waits for them, and re-layouts  1.99 us (2%)
    all_to_all x1, waiting for transfers between devices, exchange(): return lax.all_to_all(blocks, axes, split_axis=0, concat_axis=0, tiled=True)  49.2 us
    all_to_all x1, blocking collectives, exchange(): return lax.all_to_all(blocks, axes, split_axis=0, concat_axis=0, tiled=True)  14.5 us
    pallas_call x1, Pallas kernels, potential_rows(): pl.pallas_call(potential_kernel, in_specs=[pl.BlockSpec(memory_space=pltp...  13.5 us
    pallas_call x1, Pallas kernels, taylor(): pl.pallas_call(taylor_kernel, out_shape=jax.ShapeDtypeStruct(walker.shape...  4.4 us
    all_to_all x1, starting transfers between devices, exchange(): return lax.all_to_all(blocks, axes, split_axis=0, concat_axis=0, tiled=True)  2.87 us
  transfers between devices with their start and end apart: 1, of which 1 were waited for; matrix products, arithmetic and copies ran while one was open for 1% of the time, Pallas kernels for 0%

profile of v3, /device:TPU:0, one launch (start us, length us, event | category | flops | bytes accessed | tf_op | source)
XLA Modules:
  0.0 86.7 jit_solution(567417353378157613)
XLA Ops:
  0.0 0.0 copy-start
  0.0 0.8 copy-done
  0.8 0.0 copy-start.1
  0.8 0.8 copy-done.1
  1.5 0.1 shard_map.55
  1.6 14.5 %all_to_all.10 = f32[32,1,4,128]{3,2,1,0:T(4,128)S(1)} all-to-all(f32[32,1,4,128]{3,2,1,0:T(4,128)S(1)} %bitcast.13), channel_id=1, replica_groups=mesh['groups'=2,'pb'=16] {'groups','pb'}, dimensions={0} | all-to-all | bytes 131072 | tf_op jit(solution)/shard_map/all_to_all | solution.py:185
  16.1 13.5 %shard_map.56 = bf16[32,32,1024]{2,1,0:T(8,128)(2,1)} custom-call(f32[32,4,128]{2,1,0:T(4,128)S(1)} %bitcast.12, bf16[512,64,1024]{2,1,0:T(8,128)(2,1)} %slab_ref.1), custom_call_target="tpu_custom_call" | custom-call | flops 8589934592 | bytes 33554432 | tf_op jit(solution)/shard_map/pallas_call | solution.py:113
  29.6 0.0 copy-start.3
  29.7 0.0 copy-start.2
  29.7 2.9 %all-to-all-start.1 = ((bf16[32,1,32,1024]{3,2,1,0:T(8,128)(2,1)}), bf16[32,1,32,1024]{3,2,1,0:T(8,128)(2,1)S(1)}, u32[]{:S(2)}, u32[]{:S(2)}) async-start(bf16[32,1,32,1024]{3,2,1,0:T(8,128)(2,1)} %bitcast.5), calls=%async_computation.1 | async-start | bytes 4194304 | tf_op jit(solution)/shard_map/all_to_all | solution.py:185
  32.6 0.0 copy-done.3
  32.6 0.5 reshape.12.onebody_ref
  33.0 49.2 %all-to-all-done.1 = bf16[32,1,32,1024]{3,2,1,0:T(8,128)(2,1)S(1)} async-done(((bf16[32,1,32,1024]{3,2,1,0:T(8,128)(2,1)}), bf16[32,1,32,1024]{3,2,1,0:T(8,128)(2,1)S(1)}, u32[]{:S(2)}, u32[]{:S(2)}) %all-to-all-start.1) | async-done | bytes 2097184 | tf_op jit(solution)/shard_map/all_to_all | solution.py:185
  82.3 0.0 copy-done.2
  82.3 4.4 %shard_map.57 = bf16[1024,256]{1,0:T(8,128)(2,1)} custom-call(bf16[2,16,32,1024]{3,2,1,0:T(8,128)(2,1)S(1)} %bitcast.11, f32[1024,1]{1,0:T(8,128)S(1)} %reshape.12.onebody_ref, bf16[1024,256]{1,0:T(8,128)(2,1)S(1)} %bitcast.15), custom_call_target="tpu_custom_call" | custom-call | flops 2684354560 | bytes 3145728 | tf_op jit(solution)/shard_map/pallas_call | solution.py:167
Async XLA Ops:
  0.0 0.8 copy-start
  0.8 0.8 copy-start.1
  29.6 2.9 %copy-start.3 = (f32[16,64]{1,0:T(8,128)S(1)}, f32[16,64]{1,0:T(8,128)}, u32[]{:S(2)}) copy-start(f32[16,64]{1,0:T(8,128)} %param.8) | copy-start | bytes 12292
  29.7 52.6 %copy-start.2 = (bf16[1,1024,256]{2,1,0:T(8,128)(2,1)S(1)}, bf16[1,1024,256]{2,1,0:T(8,128)(2,1)}, u32[]{:S(2)}) copy-start(bf16[1,1024,256]{2,1,0:T(8,128)(2,1)} %param.9) | copy-start | bytes 1572868
  29.7 52.6 %all-to-all-start.1 = ((bf16[32,1,32,1024]{3,2,1,0:T(8,128)(2,1)}), bf16[32,1,32,1024]{3,2,1,0:T(8,128)(2,1)S(1)}, u32[]{:S(2)}, u32[]{:S(2)}) async-start(bf16[32,1,32,1024]{3,2,1,0:T(8,128)(2,1)} %bitcast.5), calls=%async_computation.1 | async-start | bytes 4194304 | tf_op jit(solution)/shard_map/all_to_all | solution.py:185

commit v4 on v3

--- a/solution.py
+++ b/solution.py
@@ -1,3 +1,5 @@
+import functools
+
 import jax
 import jax.numpy as jnp
 from jax import lax
@@ -32,7 +34,7 @@
     kpoints, vectors = field_shift.shape
     return pl.pallas_call(
         shift_kernel,
-        in_specs=[pl.BlockSpec(memory_space=pl.ANY)] * 2,
+        in_specs=[pl.BlockSpec(memory_space=pltpu.HBM)] * 2,
         out_shape=jax.ShapeDtypeStruct((copies, kpoints, vectors // LANES, LANES), jnp.float32),
         scratch_shapes=[
             pltpu.VMEM(fields.shape, jnp.float32),
@@ -40,28 +42,39 @@
             pltpu.SemaphoreType.DMA((2,)),
         ],
         compiler_params=pltpu.CompilerParams(vmem_limit_bytes=8 * MIB),
-    )(fields, field_shift)
-
-
-def potential_kernel(shifted_ref, slab_ref, out_ref, slab, left, total, arrived):
+    )(*[pltpu.with_memory_space_constraint(array, pltpu.HBM) for array in (fields, field_shift)])
+
+
+def slab_steps(vectors, rows, height):
+    steps = []
+    for top in range(0, rows, height):
+        last = [PART // 2, PART // 4, PART // 4] if top + height == rows else [PART]
+        sizes = [PART] * (vectors // PART - 1) + last
+        steps += [(top, sum(sizes[:i]), size) for i, size in enumerate(sizes)]
+    return steps
+
+
+def share_top(groups, rows):
+    return 0 if groups == 1 else pl.multiple_of(lax.axis_index("groups") * rows, rows)
+
+
+def potential_kernel(groups, steps, shifted_ref, slab_ref, out_ref, slab, left, total, arrived):
     walkers, blocks, _ = shifted_ref.shape
     vectors, rows, columns = slab.shape
-    row_blocks, parts = arrived.shape
-    height = rows // row_blocks
-    strips = height // STRIP
-    whole = rows == slab_ref.shape[1]
-    first = 0 if whole else pl.multiple_of(lax.axis_index("groups") * rows, rows)
-
-    def fetch(block, part):
+    strips = total.shape[0]
+    height = strips * STRIP
+    first = share_top(groups, rows)
+
+    def fetch(step):
+        top, vector, count = steps[step]
         return pltpu.make_async_copy(
-            slab_ref.at[pl.ds(part * PART, PART), pl.ds(first + block * height, height)],
-            slab.at[pl.ds(part * PART, PART), pl.ds(block * height, height)],
-            arrived.at[block, part],
+            slab_ref.at[pl.ds(vector, count), pl.ds(first + top, height)],
+            slab.at[pl.ds(vector, count), pl.ds(top, height)],
+            arrived.at[step],
         )
 
-    for block in range(row_blocks):
-        for part in range(parts):
-            fetch(block, part).start()
+    for step in range(len(steps)):
+        fetch(step).start()
 
     depth = LANES * STRIP
     spread = (
@@ -85,42 +98,43 @@
                 axis=0,
             ).astype(jnp.bfloat16)
 
-    for block in range(row_blocks):
-        for part in range(parts):
-            fetch(block, part).wait()
-            for strip in range(strips):
-                top = block * height + strip * STRIP
-                product = jnp.dot(
-                    left[:, part * PART * STRIP:(part + 1) * PART * STRIP],
-                    slab[part * PART:(part + 1) * PART, top:top + STRIP].reshape(PART * STRIP, columns),
-                    preferred_element_type=jnp.float32,
-                )
-                if part == 0:
-                    total[strip] = product
-                else:
-                    total[strip] += product
-        for w in range(walkers):
-            out_ref[w, block * height:(block + 1) * height] = jnp.concatenate(
-                [total[strip, w * STRIP:(w + 1) * STRIP] for strip in range(strips)], axis=0
-            ).astype(jnp.bfloat16)
+    for step, (top, vector, count) in enumerate(steps):
+        fetch(step).wait()
+        for strip in range(strips):
+            start = top + strip * STRIP
+            product = jnp.dot(
+                left[:, vector * STRIP:(vector + count) * STRIP],
+                slab[vector:vector + count, start:start + STRIP].reshape(count * STRIP, columns),
+                preferred_element_type=jnp.float32,
+            )
+            if vector == 0:
+                total[strip] = product
+            else:
+                total[strip] += product
+        if vector + count == vectors:
+            for w in range(walkers):
+                out_ref[w, top:top + height] = jnp.concatenate(
+                    [total[strip, w * STRIP:(w + 1) * STRIP] for strip in range(strips)], axis=0
+                ).astype(jnp.bfloat16)
 
 
 def potential_rows(shifted, slab, rows):
     walkers, blocks, _ = shifted.shape
-    vectors, _, columns = slab.shape
+    vectors, rows_here, columns = slab.shape
     height = min(16, rows)
+    steps = slab_steps(vectors, rows, height)
     scratch = 2 * vectors * rows * columns + 2 * walkers * STRIP * (vectors * STRIP + 2 * (height // STRIP) * columns)
     return pl.pallas_call(
-        potential_kernel,
+        functools.partial(potential_kernel, rows_here // rows, steps),
         in_specs=[pl.BlockSpec(memory_space=pltpu.VMEM), pl.BlockSpec(memory_space=pl.ANY)],
         out_shape=jax.ShapeDtypeStruct((walkers, rows, columns), jnp.bfloat16),
         scratch_shapes=[
             pltpu.VMEM((vectors, rows, columns), slab.dtype),
             pltpu.VMEM((walkers * STRIP, vectors * STRIP), jnp.bfloat16),
             pltpu.VMEM((height // STRIP, walkers * STRIP, columns), jnp.float32),
-            pltpu.SemaphoreType.DMA((rows // height, vectors // PART)),
+            pltpu.SemaphoreType.DMA((len(steps),)),
         ],
-        compiler_params=pltpu.CompilerParams(vmem_limit_bytes=scratch + 10 * MIB),
+        compiler_params=pltpu.CompilerParams(vmem_limit_bytes=scratch + 8 * MIB),
         cost_estimate=pl.CostEstimate(
             flops=2 * walkers * STRIP * rows * vectors * columns,
             bytes_accessed=2 * rows * vectors * columns,
@@ -129,12 +143,17 @@
     )(shifted, slab)
 
 
-def taylor_kernel(blocks_ref, onebody_ref, walker_ref, out_ref, matrix, diagonal, terms):
+def taylor_kernel(blocks_ref, onebody_ref, walker_ref, out_ref, matrix, diagonal, terms, result, sent):
     shares, kpoints, rows, size = blocks_ref.shape
     orbitals = size // kpoints
     columns = walker_ref.shape[1]
     per_tile = LANES // orbitals
-    for k in range(kpoints):
+    own = (
+        lax.broadcasted_iota(jnp.int32, (orbitals, orbitals), 0)
+        == lax.broadcasted_iota(jnp.int32, (orbitals, orbitals), 1)
+    )
+
+    def arrange(k):
         lanes = slice(k * orbitals, (k + 1) * orbitals)
         for tile in range(kpoints // per_tile):
             sources = [(k - tile * per_tile - i) % kpoints for i in range(per_tile)]
@@ -143,11 +162,20 @@
                 matrix[top:top + rows, tile * LANES:(tile + 1) * LANES] = jnp.concatenate(
                     [blocks_ref[s, q, :, lanes] for q in sources], axis=1
                 )
-    diagonal[...] = jnp.broadcast_to(onebody_ref[...], diagonal.shape)
+        column = jnp.sum(jnp.where(own, onebody_ref[k:k + 1], 0.0), axis=1, keepdims=True)
+        diagonal[lanes] = jnp.broadcast_to(column, (orbitals, LANES))
+
+    def send(first):
+        band = pl.ds(first * orbitals, BAND * orbitals)
+        return pltpu.make_async_copy(result.at[band], out_ref.at[band], sent.at[first // BAND])
+
     for order in range(1, TERMS):
         before = walker_ref if order == 1 else terms.at[order - 2]
         for first in range(0, kpoints, BAND):
             band = slice(first * orbitals, (first + BAND) * orbitals)
+            if order == 1:
+                for k in range(first, first + BAND):
+                    arrange(k)
             product = jnp.dot(matrix[band], before[...], preferred_element_type=jnp.float32)
             here = before[band].astype(jnp.float32)
             product += jnp.concatenate([diagonal[band]] * (columns // LANES), axis=1) * here
@@ -158,19 +186,25 @@
                 total = walker_ref[band].astype(jnp.float32)
                 for n in range(TERMS - 2):
                     total += terms[n, band].astype(jnp.float32)
-                out_ref[band] = (total + value.astype(jnp.float32)).astype(jnp.bfloat16)
+                result[band] = (total + value.astype(jnp.float32)).astype(jnp.bfloat16)
+                send(first).start()
+    for first in range(0, kpoints, BAND):
+        send(first).wait()
 
 
 def taylor(blocks, onebody, walker):
-    kpoints, orbitals = onebody.shape
+    kpoints, _ = onebody.shape
     size, columns = walker.shape
     return pl.pallas_call(
         taylor_kernel,
+        out_specs=pl.BlockSpec(memory_space=pl.ANY),
         out_shape=jax.ShapeDtypeStruct(walker.shape, jnp.bfloat16),
         scratch_shapes=[
             pltpu.VMEM((size, size), jnp.bfloat16),
             pltpu.VMEM((size, LANES), jnp.float32),
             pltpu.VMEM((TERMS - 2, size, columns), jnp.bfloat16),
+            pltpu.VMEM((size, columns), jnp.bfloat16),
+            pltpu.SemaphoreType.DMA((kpoints // BAND,)),
         ],
         compiler_params=pltpu.CompilerParams(vmem_limit_bytes=24 * MIB),
         cost_estimate=pl.CostEstimate(
@@ -178,7 +212,7 @@
             bytes_accessed=2 * size * (size + 2 * columns),
             transcendentals=0,
         ),
-    )(blocks, onebody.reshape(size, 1), walker)
+    )(blocks, onebody, walker)
 
 
 def exchange(blocks, axes):

time: 87 us -> 84 us (0.966)
  blocking collectives: 14.5 us -> 66.1 us
  waiting for transfers between devices: 49.2 us -> 0 us
  starting transfers between devices: 2.87 us -> 0 us
  local copies, waits for them, and re-layouts: 1.99 us -> 0.01 us
    all_to_all x1 -> x2, blocking collectives: 14.5 us -> 66.1 us  [exchange(): return lax.all_to_all(blocks, axes, split_axis=0, concat_axis=0, tiled=True)]
    all_to_all x1 -> x0, waiting for transfers between devices: 49.2 us -> none  [exchange(): return lax.all_to_all(blocks, axes, split_axis=0, concat_axis=0, tiled=True)]
    all_to_all x1 -> x0, starting transfers between devices: 2.87 us -> none  [exchange(): return lax.all_to_all(blocks, axes, split_axis=0, concat_axis=0, tiled=True)]
    unnamed x8 -> x4, local copies, waits for them, and re-layouts: 1.53 us -> 0.01 us
  transfers between devices with their start and end apart: 1 -> 0, of which waited for: 1 -> 0; matrix products, arithmetic and copies ran while one was open for 1% -> 0% of each run, Pallas kernels for 0% -> 0%
where the time goes in v4:
time: 84 us; the launch traced here: 83.8 us
  blocking collectives  66.1 us (79%)
  Pallas kernels  17.7 us (21%)
    all_to_all x2, blocking collectives, exchange(): return lax.all_to_all(blocks, axes, split_axis=0, concat_axis=0, tiled=True)  66.1 us
    pallas_call x1, Pallas kernels, potential_rows(): pl.pallas_call(functools.partial(potential_kernel, rows_here // rows, ste...  12.3 us
    pallas_call x1, Pallas kernels, taylor(): pl.pallas_call(taylor_kernel, out_specs=pl.BlockSpec(memory_space=pl.ANY)...  4.58 us

profile of v4, /device:TPU:0, one launch (start us, length us, event | category | flops | bytes accessed | tf_op | source)
XLA Modules:
  0.0 83.8 jit_solution(8382373236320559624)
XLA Ops:
  0.0 0.8 shard_map.55
  0.8 14.5 %all_to_all.10 = f32[32,1,4,128]{3,2,1,0:T(4,128)S(1)} all-to-all(f32[32,1,4,128]{3,2,1,0:T(4,128)S(1)} %bitcast.14), channel_id=1, replica_groups=mesh['groups'=2,'pb'=16] {'groups','pb'}, dimensions={0} | all-to-all | bytes 131072 | tf_op jit(solution)/shard_map/all_to_all | solution.py:219
  15.4 12.3 %shard_map.56 = bf16[32,32,1024]{2,1,0:T(8,128)(2,1)S(1)} custom-call(f32[32,4,128]{2,1,0:T(4,128)S(1)} %bitcast.13, bf16[512,64,1024]{2,1,0:T(8,128)(2,1)} %slab_ref.1), custom_call_target="tpu_custom_call" | custom-call | flops 8589934592 | bytes 33554432 | tf_op jit(solution)/shard_map/pallas_call | solution.py:127
  27.6 0.0 copy-start
  27.6 0.0 copy-start.1
  27.7 51.5 %all_to_all.11 = bf16[32,1,32,1024]{3,2,1,0:T(8,128)(2,1)S(1)} all-to-all(bf16[32,1,32,1024]{3,2,1,0:T(8,128)(2,1)S(1)} %bitcast.11), channel_id=1, replica_groups=mesh['groups'=2,'pb'=16] {'groups','pb'}, dimensions={0} | all-to-all | bytes 4194304 | tf_op jit(solution)/shard_map/all_to_all | solution.py:219
  79.2 0.0 copy-done
  79.2 0.0 copy-done.1
  79.2 4.6 %shard_map.57 = bf16[1024,256]{1,0:T(8,128)(2,1)} custom-call(bf16[2,16,32,1024]{3,2,1,0:T(8,128)(2,1)S(1)} %bitcast.12, f32[16,64]{1,0:T(8,128)S(1)} %copy-done.1, bf16[1024,256]{1,0:T(8,128)(2,1)S(1)} %bitcast.15), custom_call_target="tpu_custom_call" | custom-call | flops 2684354560 | bytes 3145728 | tf_op jit(solution)/shard_map/pallas_call | solution.py:198
Async XLA Ops:
  27.6 51.6 %copy-start = (bf16[1,1024,256]{2,1,0:T(8,128)(2,1)S(1)}, bf16[1,1024,256]{2,1,0:T(8,128)(2,1)}, u32[]{:S(2)}) copy-start(bf16[1,1024,256]{2,1,0:T(8,128)(2,1)} %param.9) | copy-start | bytes 1572868
  27.6 51.6 %copy-start.1 = (f32[16,64]{1,0:T(8,128)S(1)}, f32[16,64]{1,0:T(8,128)}, u32[]{:S(2)}) copy-start(f32[16,64]{1,0:T(8,128)} %onebody_ref.1) | copy-start | bytes 12292

commit v5 on v4

--- a/solution.py
+++ b/solution.py
@@ -25,9 +25,9 @@
     for copy in copies:
         copy.wait()
     shifted = (fields[...] + shift[...]).astype(jnp.bfloat16).astype(jnp.float32)
-    for copy in range(out_ref.shape[0]):
+    for copy in range(out_ref.shape[1]):
         for v in range(out_ref.shape[2]):
-            out_ref[copy, :, v, :] = shifted[:, v * LANES:(v + 1) * LANES]
+            out_ref[:, copy, v, :] = shifted[:, v * LANES:(v + 1) * LANES]
 
 
 def shift_fields(fields, field_shift, copies):
@@ -35,7 +35,7 @@
     return pl.pallas_call(
         shift_kernel,
         in_specs=[pl.BlockSpec(memory_space=pltpu.HBM)] * 2,
-        out_shape=jax.ShapeDtypeStruct((copies, kpoints, vectors // LANES, LANES), jnp.float32),
+        out_shape=jax.ShapeDtypeStruct((kpoints, copies, vectors // LANES, LANES), jnp.float32),
         scratch_shapes=[
             pltpu.VMEM(fields.shape, jnp.float32),
             pltpu.VMEM(field_shift.shape, jnp.float32),
@@ -144,7 +144,7 @@
 
 
 def taylor_kernel(blocks_ref, onebody_ref, walker_ref, out_ref, matrix, diagonal, terms, result, sent):
-    shares, kpoints, rows, size = blocks_ref.shape
+    kpoints, shares, rows, size = blocks_ref.shape
     orbitals = size // kpoints
     columns = walker_ref.shape[1]
     per_tile = LANES // orbitals
@@ -160,7 +160,7 @@
             for s in range(shares):
                 top = k * orbitals + s * rows
                 matrix[top:top + rows, tile * LANES:(tile + 1) * LANES] = jnp.concatenate(
-                    [blocks_ref[s, q, :, lanes] for q in sources], axis=1
+                    [blocks_ref[q, s, :, lanes] for q in sources], axis=1
                 )
         column = jnp.sum(jnp.where(own, onebody_ref[k:k + 1], 0.0), axis=1, keepdims=True)
         diagonal[lanes] = jnp.broadcast_to(column, (orbitals, LANES))
@@ -227,17 +227,17 @@
     per_transfer = orbitals // rows_here
 
     shares = groups if local_walkers == 1 and per_transfer == 1 and rows_here % (16 * groups) == 0 else 1
-    axes = ("groups", "pb") if shares > 1 else "pb"
+    axes = ("pb", "groups") if shares > 1 else "pb"
     rows = rows_here // shares
     outgoing = [shift_fields(fields[w], field_shift, shares) for w in range(local_walkers)]
-    outgoing = jnp.repeat(jnp.stack(outgoing, axis=2), per_transfer, axis=1)
-    arrived = exchange(outgoing.reshape((shares * devices,) + outgoing.shape[2:]), axes)
-    arrived = arrived.reshape((shares * devices * local_walkers,) + arrived.shape[2:])
+    outgoing = jnp.repeat(jnp.stack(outgoing, axis=2), per_transfer, axis=0)
+    arrived = exchange(outgoing.reshape((devices * shares,) + outgoing.shape[2:]), axes)
+    arrived = arrived.reshape((devices * shares * local_walkers,) + arrived.shape[2:])
 
     blocks = potential_rows(arrived, cholesky, rows)
-    relayed = exchange(blocks.reshape(shares * devices, local_walkers, rows, columns), axes)
+    relayed = exchange(blocks.reshape(devices * shares, local_walkers, rows, columns), axes)
     results = [
-        taylor(relayed[:, w].reshape(shares, kpoints, per_transfer * rows, columns), onebody, walkers[w])
+        taylor(relayed[:, w].reshape(kpoints, shares, per_transfer * rows, columns), onebody, walkers[w])
         for w in range(local_walkers)
     ]
     return jnp.stack(results, axis=0)

time: 84 us -> 83.2 us (level)
  no operation moved by 1% of the time
where the time goes in v5:
time: 83.2 us; the launch traced here: 83 us
  blocking collectives  65.3 us (78%)
  Pallas kernels  17.7 us (21%)
    all_to_all x2, blocking collectives, exchange(): return lax.all_to_all(blocks, axes, split_axis=0, concat_axis=0, tiled=True)  65.3 us
    pallas_call x1, Pallas kernels, potential_rows(): pl.pallas_call(functools.partial(potential_kernel, rows_here // rows, ste...  12.3 us
    pallas_call x1, Pallas kernels, taylor(): pl.pallas_call(taylor_kernel, out_specs=pl.BlockSpec(memory_space=pl.ANY)...  4.58 us

profile of v5, /device:TPU:0, one launch (start us, length us, event | category | flops | bytes accessed | tf_op | source)
XLA Modules:
  0.0 83.0 jit_solution(2697553920575981961)
XLA Ops:
  0.0 0.8 %shard_map.55 = f32[16,2,4,128]{3,2,1,0:T(4,128)S(1)} custom-call(f32[16,512]{1,0:T(8,128)} %bitcast.16, f32[16,512]{1,0:T(8,128)} %shift_ref.1), custom_call_target="tpu_custom_call" | custom-call | tf_op jit(solution)/shard_map/pallas_call | solution.py:35
  0.8 14.7 %all_to_all.10 = f32[32,1,4,128]{3,2,1,0:T(4,128)S(1)} all-to-all(f32[32,1,4,128]{3,2,1,0:T(4,128)S(1)} %bitcast.14), channel_id=1, replica_groups=mesh['groups'=2,'pb'=16] {'pb','groups'}, dimensions={0} | all-to-all | bytes 131072 | tf_op jit(solution)/shard_map/all_to_all | solution.py:219
  15.6 12.3 %shard_map.56 = bf16[32,32,1024]{2,1,0:T(8,128)(2,1)S(1)} custom-call(f32[32,4,128]{2,1,0:T(4,128)S(1)} %bitcast.13, bf16[512,64,1024]{2,1,0:T(8,128)(2,1)} %slab_ref.1), custom_call_target="tpu_custom_call" | custom-call | flops 8589934592 | bytes 33554432 | tf_op jit(solution)/shard_map/pallas_call | solution.py:127
  27.8 0.0 copy-start
  27.8 0.0 copy-start.1
  27.9 50.6 %all_to_all.11 = bf16[32,1,32,1024]{3,2,1,0:T(8,128)(2,1)S(1)} all-to-all(bf16[32,1,32,1024]{3,2,1,0:T(8,128)(2,1)S(1)} %bitcast.11), channel_id=1, replica_groups=mesh['groups'=2,'pb'=16] {'pb','groups'}, dimensions={0} | all-to-all | bytes 4194304 | tf_op jit(solution)/shard_map/all_to_all | solution.py:219
  78.4 0.0 copy-done
  78.4 0.0 copy-done.1
  78.4 4.6 %shard_map.57 = bf16[1024,256]{1,0:T(8,128)(2,1)} custom-call(bf16[16,2,32,1024]{3,2,1,0:T(8,128)(2,1)S(1)} %bitcast.12, f32[16,64]{1,0:T(8,128)S(1)} %copy-done.1, bf16[1024,256]{1,0:T(8,128)(2,1)S(1)} %bitcast.15), custom_call_target="tpu_custom_call" | custom-call | flops 2684354560 | bytes 3145728 | tf_op jit(solution)/shard_map/pallas_call | solution.py:198
Async XLA Ops:
  27.8 50.6 %copy-start = (bf16[1,1024,256]{2,1,0:T(8,128)(2,1)S(1)}, bf16[1,1024,256]{2,1,0:T(8,128)(2,1)}, u32[]{:S(2)}) copy-start(bf16[1,1024,256]{2,1,0:T(8,128)(2,1)} %param.9) | copy-start | bytes 1572868
  27.8 50.6 %copy-start.1 = (f32[16,64]{1,0:T(8,128)S(1)}, f32[16,64]{1,0:T(8,128)}, u32[]{:S(2)}) copy-start(f32[16,64]{1,0:T(8,128)} %onebody_ref.1) | copy-start | bytes 12292

commit v6 on v5

--- a/solution.py
+++ b/solution.py
@@ -10,12 +10,12 @@
 TERMS = 6
 LANES = 128
 STRIP = 8
-PART = 128
+PART = 64
 BAND = 4
 MIB = 1024 * 1024
 
 
-def shift_kernel(fields_ref, shift_ref, out_ref, fields, shift, arrived):
+def shift_kernel(fields_ref, shift_ref, out_ref, fields, shift, spread, arrived):
     copies = [
         pltpu.make_async_copy(fields_ref, fields, arrived.at[0]),
         pltpu.make_async_copy(shift_ref, shift, arrived.at[1]),
@@ -24,10 +24,11 @@
         copy.start()
     for copy in copies:
         copy.wait()
-    shifted = (fields[...] + shift[...]).astype(jnp.bfloat16).astype(jnp.float32)
+    shifted = (fields[...] + shift[...]).astype(jnp.bfloat16)
     for copy in range(out_ref.shape[1]):
         for v in range(out_ref.shape[2]):
-            out_ref[:, copy, v, :] = shifted[:, v * LANES:(v + 1) * LANES]
+            spread[:, copy, v, :] = shifted[:, v * LANES:(v + 1) * LANES].astype(jnp.float32)
+    out_ref[...] = spread[...].astype(jnp.bfloat16)
 
 
 def shift_fields(fields, field_shift, copies):
@@ -35,10 +36,11 @@
     return pl.pallas_call(
         shift_kernel,
         in_specs=[pl.BlockSpec(memory_space=pltpu.HBM)] * 2,
-        out_shape=jax.ShapeDtypeStruct((kpoints, copies, vectors // LANES, LANES), jnp.float32),
+        out_shape=jax.ShapeDtypeStruct((kpoints, copies, vectors // LANES, LANES), jnp.bfloat16),
         scratch_shapes=[
             pltpu.VMEM(fields.shape, jnp.float32),
             pltpu.VMEM(field_shift.shape, jnp.float32),
+            pltpu.VMEM((kpoints, copies, vectors // LANES, LANES), jnp.float32),
             pltpu.SemaphoreType.DMA((2,)),
         ],
         compiler_params=pltpu.CompilerParams(vmem_limit_bytes=8 * MIB),
@@ -48,7 +50,7 @@
 def slab_steps(vectors, rows, height):
     steps = []
     for top in range(0, rows, height):
-        last = [PART // 2, PART // 4, PART // 4] if top + height == rows else [PART]
+        last = [PART // 2, PART // 2] if top + height == rows else [PART]
         sizes = [PART] * (vectors // PART - 1) + last
         steps += [(top, sum(sizes[:i]), size) for i, size in enumerate(sizes)]
     return steps
@@ -58,7 +60,7 @@
     return 0 if groups == 1 else pl.multiple_of(lax.axis_index("groups") * rows, rows)
 
 
-def potential_kernel(groups, steps, shifted_ref, slab_ref, out_ref, slab, left, total, arrived):
+def potential_kernel(groups, steps, shifted_ref, slab_ref, out_ref, slab, fields, left, total, arrived):
     walkers, blocks, _ = shifted_ref.shape
     vectors, rows, columns = slab.shape
     strips = total.shape[0]
@@ -86,8 +88,9 @@
         lax.broadcasted_iota(jnp.int32, (STRIP, depth), 1) % STRIP
         == lax.broadcasted_iota(jnp.int32, (STRIP, depth), 0)
     )
+    fields[...] = shifted_ref[...].astype(jnp.float32)
     for v in range(blocks):
-        shifted = shifted_ref[:, v, :].astype(jnp.bfloat16)
+        shifted = fields[:, v, :].astype(jnp.bfloat16)
         wide = jnp.dot(shifted, spread, preferred_element_type=jnp.float32)
         for pair in range(walkers // 2):
             left[pair * 16:pair * 16 + 16, v * depth:(v + 1) * depth] = jnp.concatenate(
@@ -130,11 +133,12 @@
         out_shape=jax.ShapeDtypeStruct((walkers, rows, columns), jnp.bfloat16),
         scratch_shapes=[
             pltpu.VMEM((vectors, rows, columns), slab.dtype),
+            pltpu.VMEM(shifted.shape, jnp.float32),
             pltpu.VMEM((walkers * STRIP, vectors * STRIP), jnp.bfloat16),
             pltpu.VMEM((height // STRIP, walkers * STRIP, columns), jnp.float32),
             pltpu.SemaphoreType.DMA((len(steps),)),
         ],
-        compiler_params=pltpu.CompilerParams(vmem_limit_bytes=scratch + 8 * MIB),
+        compiler_params=pltpu.CompilerParams(vmem_limit_bytes=scratch + (8 if rows < rows_here else 24) * MIB),
         cost_estimate=pl.CostEstimate(
             flops=2 * walkers * STRIP * rows * vectors * columns,
             bytes_accessed=2 * rows * vectors * columns,

time: 83.2 us -> 82.5 us (level)
  no operation moved by 1% of the time
where the time goes in v6:
time: 82.5 us; the launch traced here: 82.3 us
  blocking collectives  65 us (79%)
  Pallas kernels  17.2 us (21%)
    all_to_all x2, blocking collectives, exchange(): return lax.all_to_all(blocks, axes, split_axis=0, concat_axis=0, tiled=True)  65 us
    pallas_call x1, Pallas kernels, potential_rows(): pl.pallas_call(functools.partial(potential_kernel, rows_here // rows, ste...  11.8 us
    pallas_call x1, Pallas kernels, taylor(): pl.pallas_call(taylor_kernel, out_specs=pl.BlockSpec(memory_space=pl.ANY)...  4.58 us

profile of v6, /device:TPU:0, one launch (start us, length us, event | category | flops | bytes accessed | tf_op | source)
XLA Modules:
  0.0 82.3 jit_solution(5030704467097260291)
XLA Ops:
  0.0 0.8 %shard_map.55 = bf16[16,2,4,128]{3,2,1,0:T(4,128)(2,1)S(1)} custom-call(f32[16,512]{1,0:T(8,128)} %bitcast.16, f32[16,512]{1,0:T(8,128)} %shift_ref.1), custom_call_target="tpu_custom_call" | custom-call | tf_op jit(solution)/shard_map/pallas_call | solution.py:36
  0.9 14.5 %all_to_all.10 = bf16[32,1,4,128]{3,2,1,0:T(4,128)(2,1)S(1)} all-to-all(bf16[32,1,4,128]{3,2,1,0:T(4,128)(2,1)S(1)} %bitcast.14), channel_id=1, replica_groups=mesh['groups'=2,'pb'=16] {'pb','groups'}, dimensions={0} | all-to-all | bytes 65536 | tf_op jit(solution)/shard_map/all_to_all | solution.py:223
  15.3 11.8 %shard_map.56 = bf16[32,32,1024]{2,1,0:T(8,128)(2,1)S(1)} custom-call(bf16[32,4,128]{2,1,0:T(4,128)(2,1)S(1)} %bitcast.13, bf16[512,64,1024]{2,1,0:T(8,128)(2,1)} %slab_ref.1), custom_call_target="tpu_custom_call" | custom-call | flops 8589934592 | bytes 33554432 | tf_op jit(solution)/shard_map/pallas_call | solution.py:130
  27.1 0.0 copy-start
  27.1 0.0 copy-start.1
  27.1 50.6 %all_to_all.11 = bf16[32,1,32,1024]{3,2,1,0:T(8,128)(2,1)S(1)} all-to-all(bf16[32,1,32,1024]{3,2,1,0:T(8,128)(2,1)S(1)} %bitcast.11), channel_id=1, replica_groups=mesh['groups'=2,'pb'=16] {'pb','groups'}, dimensions={0} | all-to-all | bytes 4194304 | tf_op jit(solution)/shard_map/all_to_all | solution.py:223
  77.7 0.0 copy-done
  77.7 0.0 copy-done.1
  77.7 4.6 %shard_map.57 = bf16[1024,256]{1,0:T(8,128)(2,1)} custom-call(bf16[16,2,32,1024]{3,2,1,0:T(8,128)(2,1)S(1)} %bitcast.12, f32[16,64]{1,0:T(8,128)S(1)} %copy-done.1, bf16[1024,256]{1,0:T(8,128)(2,1)S(1)} %bitcast.15), custom_call_target="tpu_custom_call" | custom-call | flops 2684354560 | bytes 3145728 | tf_op jit(solution)/shard_map/pallas_call | solution.py:202
Async XLA Ops:
  27.1 50.6 %copy-start = (bf16[1,1024,256]{2,1,0:T(8,128)(2,1)S(1)}, bf16[1,1024,256]{2,1,0:T(8,128)(2,1)}, u32[]{:S(2)}) copy-start(bf16[1,1024,256]{2,1,0:T(8,128)(2,1)} %param.9) | copy-start | bytes 1572868
  27.1 50.6 %copy-start.1 = (f32[16,64]{1,0:T(8,128)S(1)}, f32[16,64]{1,0:T(8,128)}, u32[]{:S(2)}) copy-start(f32[16,64]{1,0:T(8,128)} %onebody_ref.1) | copy-start | bytes 12292

commit v7 on v6

--- a/solution.py
+++ b/solution.py
@@ -157,6 +157,18 @@
         == lax.broadcasted_iota(jnp.int32, (orbitals, orbitals), 1)
     )
 
+    turned = {}
+
+    def piece(q, s, k, place):
+        tile, at = divmod(k, per_tile)
+        lanes = slice(tile * LANES, (tile + 1) * LANES)
+        shift = (place - at) % per_tile * orbitals
+        key = (q, s, tile, shift)
+        if key not in turned:
+            block = blocks_ref[q, s, :, lanes]
+            turned[key] = jnp.concatenate([block[:, LANES - shift:], block[:, :LANES - shift]], axis=1) if shift else block
+        return turned[key][:, place * orbitals:(place + 1) * orbitals]
+
     def arrange(k):
         lanes = slice(k * orbitals, (k + 1) * orbitals)
         for tile in range(kpoints // per_tile):
@@ -164,7 +176,7 @@
             for s in range(shares):
                 top = k * orbitals + s * rows
                 matrix[top:top + rows, tile * LANES:(tile + 1) * LANES] = jnp.concatenate(
-                    [blocks_ref[q, s, :, lanes] for q in sources], axis=1
+                    [piece(q, s, k, place) for place, q in enumerate(sources)], axis=1
                 )
         column = jnp.sum(jnp.where(own, onebody_ref[k:k + 1], 0.0), axis=1, keepdims=True)
         diagonal[lanes] = jnp.broadcast_to(column, (orbitals, LANES))

time: 82.5 us -> 82.3 us (level)
  no operation moved by 1% of the time
where the time goes in v7:
time: 82.3 us; the launch traced here: 82 us
  blocking collectives  65 us (79%)
  Pallas kernels  17 us (21%)
    all_to_all x2, blocking collectives, exchange(): return lax.all_to_all(blocks, axes, split_axis=0, concat_axis=0, tiled=True)  65 us
    pallas_call x1, Pallas kernels, potential_rows(): pl.pallas_call(functools.partial(potential_kernel, rows_here // rows, ste...  11.8 us
    pallas_call x1, Pallas kernels, taylor(): pl.pallas_call(taylor_kernel, out_specs=pl.BlockSpec(memory_space=pl.ANY)...  4.32 us

profile of v7, /device:TPU:0, one launch (start us, length us, event | category | flops | bytes accessed | tf_op | source)
XLA Modules:
  0.0 82.0 jit_solution(8485622314728773709)
XLA Ops:
  0.0 0.8 %shard_map.55 = bf16[16,2,4,128]{3,2,1,0:T(4,128)(2,1)S(1)} custom-call(f32[16,512]{1,0:T(8,128)} %bitcast.16, f32[16,512]{1,0:T(8,128)} %shift_ref.1), custom_call_target="tpu_custom_call" | custom-call | tf_op jit(solution)/shard_map/pallas_call | solution.py:36
  0.9 14.5 %all_to_all.10 = bf16[32,1,4,128]{3,2,1,0:T(4,128)(2,1)S(1)} all-to-all(bf16[32,1,4,128]{3,2,1,0:T(4,128)(2,1)S(1)} %bitcast.14), channel_id=1, replica_groups=mesh['groups'=2,'pb'=16] {'pb','groups'}, dimensions={0} | all-to-all | bytes 65536 | tf_op jit(solution)/shard_map/all_to_all | solution.py:235
  15.3 11.8 %shard_map.56 = bf16[32,32,1024]{2,1,0:T(8,128)(2,1)S(1)} custom-call(bf16[32,4,128]{2,1,0:T(4,128)(2,1)S(1)} %bitcast.13, bf16[512,64,1024]{2,1,0:T(8,128)(2,1)} %slab_ref.1), custom_call_target="tpu_custom_call" | custom-call | flops 8589934592 | bytes 33554432 | tf_op jit(solution)/shard_map/pallas_call | solution.py:130
  27.1 0.0 copy-start
  27.1 0.0 copy-start.1
  27.1 50.6 %all_to_all.11 = bf16[32,1,32,1024]{3,2,1,0:T(8,128)(2,1)S(1)} all-to-all(bf16[32,1,32,1024]{3,2,1,0:T(8,128)(2,1)S(1)} %bitcast.11), channel_id=1, replica_groups=mesh['groups'=2,'pb'=16] {'pb','groups'}, dimensions={0} | all-to-all | bytes 4194304 | tf_op jit(solution)/shard_map/all_to_all | solution.py:235
  77.7 0.0 copy-done
  77.7 0.0 copy-done.1
  77.7 4.3 %shard_map.57 = bf16[1024,256]{1,0:T(8,128)(2,1)} custom-call(bf16[16,2,32,1024]{3,2,1,0:T(8,128)(2,1)S(1)} %bitcast.12, f32[16,64]{1,0:T(8,128)S(1)} %copy-done.1, bf16[1024,256]{1,0:T(8,128)(2,1)S(1)} %bitcast.15), custom_call_target="tpu_custom_call" | custom-call | flops 2684354560 | bytes 3145728 | tf_op jit(solution)/shard_map/pallas_call | solution.py:214
Async XLA Ops:
  27.1 50.6 %copy-start = (bf16[1,1024,256]{2,1,0:T(8,128)(2,1)S(1)}, bf16[1,1024,256]{2,1,0:T(8,128)(2,1)}, u32[]{:S(2)}) copy-start(bf16[1,1024,256]{2,1,0:T(8,128)(2,1)} %param.9) | copy-start | bytes 1572868
  27.1 50.6 %copy-start.1 = (f32[16,64]{1,0:T(8,128)S(1)}, f32[16,64]{1,0:T(8,128)}, u32[]{:S(2)}) copy-start(f32[16,64]{1,0:T(8,128)} %onebody_ref.1) | copy-start | bytes 12292
